TPU v7x, 32 devices: a whole 2x2x4 slice. The times are simulated.
32 devices in a mesh: dp: 2 (over y), expert: 16 (over z, x, core).
Axes of the slice: x: 2, y: 2, z: 4, core: 2. Of those that a mesh axis runs over, the one named last changes fastest.
Arguments:
- hidden_rows: bfloat16 [768, 4096], P(None, ('dp', 'expert')), may hold values from -6 to 6
- grad_rows: bfloat16 [4096, 2560], P(('dp', 'expert')), may hold values from -0.1796875 to 0.1796875
- block_slot: int32 [32, 1], P(('dp', 'expert')), may hold values from 0 to 1
- live_rows: int32 [32], P(('dp', 'expert')), may hold values from 16 to 128
- replica_plan: int32 [16], replicated, may hold values from 0 to 3
- master: float32 [16, 768, 640], P('expert', 'dp'), may hold values from -0.21875 to 0.21875
- moment_one: float32 [16, 768, 640], P('expert', 'dp'), may hold values from -1.8 to 1.8
- moment_two: float32 [16, 768, 640], P('expert', 'dp'), may hold values from 0.01 to 1
Outputs:
- master_new: float32 [16, 768, 640], P('expert', 'dp')
- first_new: float32 [16, 768, 640], P('expert', 'dp')
- second_new: float32 [16, 768, 640], P('expert', 'dp')
- replica_weight: bfloat16 [16, 768, 2560], P('expert', 'dp')
Inputs may be any that keep to these rules, and one draw needn't show every extreme that they name: replica_plan[j] is the expert of which the devices at index j along the expert axis host a replica; it may equal j mod 4. `block_slot`: 0 marks a block of the primary expert, 1 a block of the replica.
All inputs are finite; a program needn't handle non-finite values.
Results may differ from a plain program's by a relative error of at most 0.001.
Values may be sent and summed in bfloat16 or wider, within the bound.
No kernel may reach another device: no remote copies, remote signals or barrier semaphores. Data moves between devices by JAX's collectives and lax.ppermute only.
A program may use at most 64 MiB of HBM per device.

v0:
```python
import functools

import jax
import jax.numpy as jnp
from jax import lax
from jax.experimental import pallas as pl
from jax.experimental.pallas import tpu as pltpu
from jax.sharding import PartitionSpec as P

QUART = 4
LANES = 128
META_ROWS = 16


beta_one = 0.9
beta_two = 0.95
learn_rate = 0.01
decay_rate = 0.1
epsilon = 1e-08
step_count = 10.0

VMEM = pl.BlockSpec(memory_space=pltpu.VMEM)
SMEM = pl.BlockSpec(memory_space=pltpu.SMEM)
ANYWHERE = pl.BlockSpec(memory_space=pl.ANY)


def vmem_for(*arrays):
    return int(sum(a.size * a.dtype.itemsize for a in arrays) * 5 // 4) + (8 << 20)


def call(kernel, out_shapes, scalars, arrays, flops=0):
    moved = sum(a.size * a.dtype.itemsize for a in (*arrays, *out_shapes))
    return pl.pallas_call(
        kernel,
        out_shape=tuple(out_shapes),
        in_specs=[SMEM] * len(scalars) + [VMEM] * len(arrays),
        out_specs=tuple([VMEM] * len(out_shapes)),
        compiler_params=pltpu.CompilerParams(vmem_limit_bytes=vmem_for(*arrays, *out_shapes)),
        cost_estimate=pl.CostEstimate(flops=flops // 64, bytes_accessed=moved // 64, transcendentals=0),
    )(*scalars, *arrays)


def from_behind(block, axis, distance):
    devices = range(lax.axis_size(axis))
    route = [((i - distance) % len(devices), i) for i in devices]
    return lax.ppermute(block, axis, route)


def from_mate(block, axis, bit):
    return lax.ppermute(block, axis, [(i ^ bit, i) for i in range(lax.axis_size(axis))])


def gather_mates(block, axis, count, least=1):
    held = {0: block}
    bit = count // 2
    while bit >= least:
        held.update({m | bit: from_mate(held[m], axis, bit) for m in list(held)})
        bit //= 2
    return [held.get(m) for m in range(count)]


def after(value, *others):
    return lax.optimization_barrier((value, *others))[0] if others else value


def exchange(packs, bit):
    keys = [(step, mate | bit) for pack, _ in packs for step, mate in pack]
    blocks = [block for _, block in packs]
    return keys, from_mate(jnp.concatenate(blocks) if len(blocks) > 1 else blocks[0], "expert", bit)


def places(packs, first):
    found = {}
    for at, (keys, block) in enumerate(packs):
        rows = block.shape[0] // len(keys)
        found.update({key: (first + at, i * rows) for i, key in enumerate(keys)})
    return found


def place(owner_count):
    own = lax.axis_index("expert")
    return own // owner_count, own % owner_count


def message_kernel(owner_count, spans, slot_ref, live_ref, hidden_ref, grad_ref, *message_refs):
    own_block, _ = place(owner_count)
    groups = lax.axis_size("dp")
    hidden_units, tok_rows = hidden_ref.shape
    share_rows = hidden_units // groups
    block_width = grad_ref.shape[1] // QUART
    parts = block_width // LANES
    live = live_ref[0]
    slot = slot_ref[0, 0]
    kept = lax.broadcasted_iota(jnp.int32, (tok_rows, LANES), 0) < live
    meta = jnp.full((META_ROWS, LANES), slot.astype(jnp.float32)).astype(jnp.bfloat16)

    def put_hidden(message, row, span):
        first, length = span
        for group in range(groups):
            start = group * share_rows + first
            message[row : row + length, :] = hidden_ref[start : start + length, :]
            row += length

    for step, message in enumerate(message_refs[:QUART]):
        target = lax.rem(own_block + step, QUART)
        for part in range(parts):
            start = pl.multiple_of(target * block_width + part * LANES, LANES)
            columns = grad_ref[:, pl.ds(start, LANES)].astype(jnp.float32)
            row = part * tok_rows
            message[row : row + tok_rows, :] = jnp.where(kept, columns, 0.0).astype(jnp.bfloat16)
        row = parts * tok_rows
        message[row : row + META_ROWS, :] = meta
        put_hidden(message, row + META_ROWS, spans[0])
    for message, span in zip(message_refs[QUART:], spans[1:]):
        put_hidden(message, 0, span)


def partial_kernel(owner_count, tok_rows, where, base, steps, plan_ref, *refs):
    totals = refs[-len(steps) :]
    own_block, own_expert = place(owner_count)
    group, groups = lax.axis_index("dp"), lax.axis_size("dp")
    rows, block_width = totals[0].shape
    parts = block_width // LANES
    chunk = next(c for c in (208, 192, 176, 128, 112, 96, 64, 48, 32, 16) if rows % c == 0)
    bits = []
    for first in range(0, len(where), 16):
        packed = jnp.zeros((META_ROWS, LANES), jnp.float32)
        for at, (_, (head, row), _) in enumerate(where[first : first + 16]):
            meta = refs[head][row + parts * tok_rows : row + parts * tok_rows + META_ROWS, :]
            packed = packed + meta.astype(jnp.float32) * float(1 << at)
        bits.append(jnp.max(packed).astype(jnp.int32))
    for total in totals:
        total[...] = jnp.zeros_like(total)
    for at, ((step, mate), (head, head_row), (tail, tail_row)) in enumerate(where):
        source_expert = own_expert ^ mate
        source = lax.rem(own_block + QUART - step, QUART) * owner_count + source_expert
        is_replica = ((bits[at // 16] >> (at % 16)) & 1) == 1
        target = jnp.where(is_replica, plan_ref[source], source_expert)

        columns = jnp.concatenate(
            [
                refs[head][head_row + p * tok_rows : head_row + (p + 1) * tok_rows, :]
                for p in range(parts)
            ],
            axis=1,
        )

        def add(rounded):
            for total, ahead in zip(totals, steps):
                start = tail_row + base + lax.rem(group + ahead, groups) * rows

                @pl.loop(0, rows // chunk)
                def _(i):
                    term = jnp.dot(
                        refs[tail][pl.ds(pl.multiple_of(start + i * chunk, 16), chunk), :],
                        columns,
                        preferred_element_type=jnp.float32,
                    )
                    if rounded:
                        term = term.astype(jnp.bfloat16).astype(jnp.float32)
                    into = pl.ds(pl.multiple_of(i * chunk, 16), chunk)
                    total[into, :] += term

        if mate == 0:
            pl.when((target == own_expert) & jnp.logical_not(is_replica))(lambda: add(False))
        pl.when((target == own_expert) & is_replica)(lambda: add(True))


def new_rows(terms, states, first, start, size):
    inside, placed = pl.ds(start, size), pl.ds(first + start, size)
    master, one, two = states
    gradient = terms[0][inside, :]
    for term in terms[1:]:
        gradient = gradient + term[inside, :]
    weights = master[placed, :]
    first_next = beta_one * one[placed, :] + (1.0 - beta_one) * gradient
    second_next = beta_two * two[placed, :] + (1.0 - beta_two) * gradient * gradient
    scaled_first = first_next / (1.0 - beta_one**step_count)
    scaled_second = second_next / (1.0 - beta_two**step_count)
    direction = scaled_first / (jnp.sqrt(scaled_second) + epsilon)
    weights_next = weights - learn_rate * (direction + decay_rate * weights)
    return weights_next, first_next, second_next


def update_kernel(parts, first, pieces, *refs):
    terms, states, outs = refs[:parts], refs[parts : parts + 3], refs[parts + 3 :]
    for start, size in pieces:
        values = new_rows(terms, states, first, start, size)
        for out, value in zip(outs, (*values, values[0].astype(jnp.bfloat16))):
            out[pl.ds(start, size), :] = value


def finish_kernel(parts, first, pieces, *refs):
    terms, states, made = refs[:parts], refs[parts : parts + 3], refs[parts + 3 : parts + 6]
    *outs, fresh, fresh_states, sems = refs[parts + 6 :]
    copies = [
        pltpu.make_async_copy(rows, out.at[pl.ds(0, first), :], sems.at[which, 0])
        for which, (rows, out) in enumerate(zip(made, outs))
    ]
    for copy in copies:
        copy.start()
    for at, (start, size) in enumerate(pieces):
        inside, placed = pl.ds(start, size), pl.ds(first + start, size)
        values = new_rows(terms, states, first, start, size)
        fresh[inside, :] = values[0].astype(jnp.bfloat16)
        for which, value in enumerate(values):
            fresh_states[which, inside, :] = value
            copies.append(
                pltpu.make_async_copy(
                    fresh_states.at[which, inside, :],
                    outs[which].at[placed, :],
                    sems.at[which, at + 1],
                )
            )
            copies[-1].start()
    for copy in copies:
        copy.wait()


def update(terms, states, span, made=()):
    first, length = span
    rows, width = states[0].shape
    pieces = [(start, min(64, length - start)) for start in range(0, length, 64)]
    part = jax.ShapeDtypeStruct((length, width), jnp.float32)
    whole = jax.ShapeDtypeStruct((rows, width), jnp.float32)
    scratch = [
        pltpu.VMEM((3, length, width), jnp.float32),
        pltpu.SemaphoreType.DMA((3, len(pieces) + 1)),
    ]
    return pl.pallas_call(
        functools.partial(finish_kernel if made else update_kernel, len(terms), first, pieces),
        out_shape=(
            *([whole if made else part] * 3),
            jax.ShapeDtypeStruct((length, width), jnp.bfloat16),
        ),
        in_specs=[VMEM] * (len(terms) + len(states) + len(made)),
        out_specs=(*([ANYWHERE if made else VMEM] * 3), VMEM),
        scratch_shapes=scratch if made else [],
        compiler_params=pltpu.CompilerParams(vmem_limit_bytes=24 << 20),
        cost_estimate=pl.CostEstimate(
            flops=length * width, bytes_accessed=length * width, transcendentals=0
        ),
    )(*terms, *states, *made)


def choose_kernel(owner_count, plan_ref, *refs):
    candidates, chosen = refs[:owner_count], refs[owner_count:]
    own_block, own_expert = place(owner_count)
    for step, out in enumerate(chosen):
        wanted = plan_ref[lax.rem(own_block + step, QUART) * owner_count + own_expert]
        for mate, candidate in enumerate(candidates):

            @pl.when(wanted == own_expert ^ mate)
            def _():
                out[...] = candidate[...]


def offer_kernel(owner_count, plan_ref, *refs):
    held, out = refs[:-1], refs[-1]
    own_block, own_expert = place(owner_count)
    wanted = plan_ref[own_block * owner_count + (own_expert ^ 1)]
    rows = out.shape[0]
    for pair, blocks in enumerate(held):

        @pl.when((wanted ^ own_expert) >> 1 == pair)
        def _():
            for step in range(QUART):
                width = blocks.shape[1]
                column = pl.multiple_of(lax.rem(own_block + QUART - step, QUART) * width, LANES)
                out[:, pl.ds(column, width)] = blocks[step * rows : (step + 1) * rows, :]


def assemble_kernel(owner_count, span, later, plan_ref, *refs):
    *blocks, out, sems = refs
    own_block, own_expert = place(owner_count)
    apart = plan_ref[own_block * owner_count + own_expert] ^ own_expert
    first, rows = span
    half = owner_count // 2

    def put(sources, start, group):
        copies = []
        for step, source in enumerate(sources):
            width = source.shape[1]
            column = pl.multiple_of(lax.rem(own_block + QUART - step, QUART) * width, LANES)
            target = out.at[pl.ds(start, source.shape[0]), pl.ds(column, width)]
            copies.append(pltpu.make_async_copy(source, target, sems.at[group, step]))
            copies[-1].start()
        return copies

    def finish(copies):
        for copy in copies:
            copy.wait()

    if later:
        offered, _ = blocks

        @pl.when(apart & 1 == 1)
        def _():
            copy = pltpu.make_async_copy(offered, out.at[pl.ds(first, rows), :], sems.at[0, 0])
            copy.start()
            copy.wait()

        return

    held, received = blocks[:half], blocks[half:]
    others = put(received, first + rows, 0)
    for pair in range(half):

        @pl.when(apart == 2 * pair)
        def _():
            lines = [held[pair].at[pl.ds(step * rows, rows), :] for step in range(QUART)]
            finish(put(lines, first, 1))

    finish(others)


def assemble(owner_count, span, plan, blocks, shape, held=None):
    later = held is not None
    inputs = [*blocks, held] if later else blocks
    return pl.pallas_call(
        functools.partial(assemble_kernel, owner_count, span, later),
        out_shape=shape,
        in_specs=[SMEM] + [VMEM] * len(blocks) + [ANYWHERE] * later,
        out_specs=ANYWHERE,
        scratch_shapes=[pltpu.SemaphoreType.DMA((2, QUART))],
        input_output_aliases={1 + len(blocks): 0} if later else {},
        compiler_params=pltpu.CompilerParams(vmem_limit_bytes=vmem_for(*blocks)),
        cost_estimate=pl.CostEstimate(flops=1, bytes_accessed=1 << 14, transcendentals=0),
    )(plan, *inputs)


def per_device(
    hidden_rows, grad_rows, block_slot, live_rows, replica_plan, master, moment_one, moment_two
):
    owner_count = lax.axis_size("expert") // QUART
    groups = lax.axis_size("dp")
    hidden_units, tok_rows = hidden_rows.shape
    block_width = grad_rows.shape[1] // QUART
    share_rows = hidden_units // groups
    assert block_slot.shape[1] == 1 and tok_rows == LANES and block_width % LANES == 0
    shape = jax.ShapeDtypeStruct
    lead = share_rows * 13 // 24 // 16 * 16
    spans = ((0, lead), (lead, share_rows - lead))

    head_rows = (block_width // LANES) * tok_rows + META_ROWS
    outs = [shape((head_rows + groups * lead, LANES), jnp.bfloat16)] * QUART
    outs += [shape((groups * (share_rows - lead), LANES), jnp.bfloat16)]
    messages = call(
        functools.partial(message_kernel, owner_count, spans),
        outs,
        (block_slot, live_rows),
        (hidden_rows, grad_rows),
    )

    def across(block, step):
        return from_behind(block, "expert", step * owner_count) if step else block

    first_bit = owner_count // 2
    other_bits = [1 << i for i in reversed(range(first_bit.bit_length() - 1))]
    own = [([(0, 0)], messages[0])]
    sides = [([(step, 0)], across(messages[step], step)) for step in (1, 3)]
    keys, block = exchange(own, first_bit)
    own += [(keys, after(block, *(side for _, side in sides))), *sides]
    last = [([(2, 0)], across(after(messages[2], own[1][1]), 2))]
    crossed = [exchange(sides, first_bit)]
    last_crossed = exchange(last, first_bit)
    for bit in other_bits:
        own += [exchange(own, bit)]
        last += [exchange(last, bit)]
    later = after(messages[QUART], last[-1][1], crossed[0][1])
    rest = [([(0, 0)], messages[QUART])]
    rest += [([(step, 0)], across(later, step)) for step in (1, 2, 3)]
    keys, block = last_crossed
    crossed += [(keys, after(block, *(part for _, part in rest[1:])))]
    for bit in other_bits:
        crossed += [exchange(crossed, bit)]
    last += crossed
    heads = own + last
    head_at = places(heads, 0)
    rests, rest_at = [], {}

    def partials(at, steps, wait_for):
        rows = spans[at][1]
        packs = heads + rests if at else heads
        where = [(key, found, rest_at[key] if at else found) for key, found in head_at.items()]
        return call(
            functools.partial(
                partial_kernel, owner_count, tok_rows, where, 0 if at else head_rows, steps
            ),
            [shape((rows, block_width), jnp.float32)] * len(steps),
            (after(replica_plan, *wait_for),),
            [block for _, block in packs],
            2 * len(steps) * rows * tok_rows * block_width * QUART,
        )

    states = (master[0], moment_one[0], moment_two[0])
    ahead = tuple(range(1, groups))
    block = lambda rows: shape((rows, block_width), jnp.bfloat16)

    far_one = partials(0, ahead, ())
    came_one = [from_behind(p, "dp", step) for step, p in zip(ahead, far_one)]
    near_one = partials(0, (0,), far_one)

    keys, parts = zip(*rest)
    stack = jnp.concatenate(parts)
    rest = [(sum(keys, []), stack)]
    rest += [exchange(rest, first_bit)]
    for pack in rest:
        group = [pack]
        for bit in other_bits:
            group += [exchange(group, bit)]
        rests += group
    rest_at.update(places(rests, len(heads)))

    far_two = partials(1, ahead, near_one)
    came_one = [after(term, *far_two) for term in came_one]
    *made, fresh_one = update((*near_one, *came_one), states, spans[0])
    came_two = [
        from_behind(after(p, fresh_one), "dp", step) for step, p in zip(ahead, far_two)
    ]
    near_two = partials(1, (0,), (fresh_one,))

    lines = [across(fresh_one, step) for step in range(QUART)]

    came_two = [after(term, fresh_one) for term in came_two]
    *held, fresh_two = update((*near_two, *came_two), states, spans[1], made)

    mates_two = gather_mates(fresh_two, "expert", owner_count)
    lines[1:] = [after(line, mates_two[owner_count // 2]) for line in lines[1:]]
    chosen = call(
        functools.partial(choose_kernel, owner_count),
        [block(spans[1][1])] * QUART,
        (after(replica_plan, *lines),),
        mates_two,
    )
    received = [across(c, step) for step, c in enumerate(chosen)]

    wide = gather_mates(jnp.concatenate(lines), "expert", owner_count, 2)[::2]
    (offer,) = call(
        functools.partial(offer_kernel, owner_count),
        [shape((spans[0][1], QUART * block_width), jnp.bfloat16)],
        (replica_plan,),
        wide,
    )
    result = shape((share_rows, QUART * block_width), jnp.bfloat16)
    placed = assemble(
        owner_count, spans[0], replica_plan, [*wide, *received], result
    )
    offer = from_mate(after(offer, *received[1:]), "expert", 1)
    replica_weight = assemble(owner_count, spans[0], replica_plan, [offer], result, placed)
    return (*(state[None] for state in held), replica_weight[None])


def solution(mesh):
    return jax.shard_map(
        per_device,
        mesh=mesh,
        in_specs=(
            P(None, ("dp", "expert")),
            P(("dp", "expert"), None),
            P(("dp", "expert"), None),
            P(("dp", "expert")),
            P(),
            P("expert", "dp", None),
            P("expert", "dp", None),
            P("expert", "dp", None),
        ),
        out_specs=(
            P("expert", "dp", None),
            P("expert", "dp", None),
            P("expert", "dp", None),
            P("expert", "dp", None),
        ),
        check_vma=False,
    )
```

profile of v0, /device:TPU:9, one launch (start us, length us, event | category | flops | bytes accessed | tf_op | source)
XLA Modules:
  0.0 122.6 jit_solution(14837612487701206493)
XLA Ops:
  1.9 1.1 copy-done.3
  3.0 0.9 copy-done.4
  4.1 1.3 %collective-permute-start.1 = (bf16[1072,128]{1,0:T(8,128)(2,1)S(1)}, bf16[1072,128]{1,0:T(8,128)(2,1)S(1)}, u32[]{:S(2)}, u32[]{:S(2)}) collective-permute-start(bf16[1072,128]{1,0:T(8,128)(2,1)S(1)} %get-tuple-element.37), channel_id=1, source_target_pairs={{12,0},{13,1},{14,2},{15,3},{0,4},{1,5},{2,6},{3,7},{4,8},{5,9},{6... | collective-permute-start | bytes 823304 | tf_op jit(solution)/shard_map/ppermute | solution.py:46
  5.6 1.2 collective-permute-start
  6.8 4.8 %collective-permute-done.1.refs_2_ = bf16[1072,128]{1,0:T(8,128)(2,1)S(1)} collective-permute-done((bf16[1072,128]{1,0:T(8,128)(2,1)S(1)}, bf16[1072,128]{1,0:T(8,128)(2,1)S(1)}, u32[]{:S(2)}, u32[]{:S(2)}) %collective-permute-start.1) | collective-permute-done | bytes 274464 | tf_op jit(solution)/shard_map/ppermute | solution.py:46
  11.6 7.8 %collective-permute-done.2.refs_3_ = bf16[1072,128]{1,0:T(8,128)(2,1)S(1)} collective-permute-done((bf16[1072,128]{1,0:T(8,128)(2,1)S(1)}, bf16[1072,128]{1,0:T(8,128)(2,1)S(1)}, u32[]{:S(2)}, u32[]{:S(2)}) %collective-permute-start.2) | collective-permute-done | bytes 274464 | tf_op jit(solution)/shard_map/ppermute | solution.py:46
  19.6 1.3 %collective-permute-start.6 = (bf16[2144,128]{1,0:T(8,128)(2,1)S(1)}, bf16[2144,128]{1,0:T(8,128)(2,1)S(1)}, u32[]{:S(2)}, u32[]{:S(2)}) collective-permute-start(bf16[2144,128]{1,0:T(8,128)(2,1)S(1)} %pad_maximum_fusion.2), channel_id=1, source_target_pairs={{2,0},{3,1},{0,2},{1,3},{6,4},{7,5},{4,6},{5,7},{10,8},{11,9},{8,1... | collective-permute-start | bytes 1646600 | tf_op jit(solution)/shard_map/ppermute | solution.py:50
  20.9 10.5 %collective-permute-done.4.refs_5_ = bf16[1072,128]{1,0:T(8,128)(2,1)S(1)} collective-permute-done((bf16[1072,128]{1,0:T(8,128)(2,1)S(1)}, bf16[1072,128]{1,0:T(8,128)(2,1)S(1)}, u32[]{:S(2)}, u32[]{:S(2)}) %collective-permute-start.4) | collective-permute-done | bytes 274464 | tf_op jit(solution)/shard_map/ppermute | solution.py:46
  31.4 0.8 collective-permute-start.5
  32.3 1.2 collective-permute-start.7
  33.5 2.9 %collective-permute-start.10 = (bf16[352,128]{1,0:T(8,128)(2,1)S(1)}, bf16[352,128]{1,0:T(8,128)(2,1)S(1)}, u32[]{:S(2)}, u32[]{:S(2)}) collective-permute-start(bf16[352,128]{1,0:T(8,128)(2,1)S(1)} %get-tuple-element.43), channel_id=1, source_target_pairs={{4,0},{5,1},{6,2},{7,3},{8,4},{9,5},{10,6},{11,7},{12,8},{13,9},{1... | collective-permute-start | bytes 270344 | tf_op jit(solution)/shard_map/ppermute | solution.py:46
  36.7 2.3 %collective-permute-start.8 = (bf16[352,128]{1,0:T(8,128)(2,1)S(1)}, bf16[352,128]{1,0:T(8,128)(2,1)S(1)}, u32[]{:S(2)}, u32[]{:S(2)}) collective-permute-start(bf16[352,128]{1,0:T(8,128)(2,1)S(1)} %get-tuple-element.43), channel_id=1, source_target_pairs={{12,0},{13,1},{14,2},{15,3},{0,4},{1,5},{2,6},{3,7},{4,8},{5,9},{6... | collective-permute-start | bytes 270344 | tf_op jit(solution)/shard_map/ppermute | solution.py:46
  39.0 1.2 %collective-permute-start.3 = (bf16[4288,128]{1,0:T(8,128)(2,1)S(1)}, bf16[4288,128]{1,0:T(8,128)(2,1)S(1)}, u32[]{:S(2)}, u32[]{:S(2)}) collective-permute-start(bf16[4288,128]{1,0:T(8,128)(2,1)S(1)} %pad_maximum_fusion), channel_id=1, source_target_pairs={{1,0},{0,1},{3,2},{2,3},{5,4},{4,5},{7,6},{6,7},{9,8},{8,9},{11,10... | collective-permute-start | bytes 3293192 | tf_op jit(solution)/shard_map/ppermute | solution.py:50
  40.7 3.4 %collective-permute-done.8 = bf16[352,128]{1,0:T(8,128)(2,1)S(1)} collective-permute-done((bf16[352,128]{1,0:T(8,128)(2,1)S(1)}, bf16[352,128]{1,0:T(8,128)(2,1)S(1)}, u32[]{:S(2)}, u32[]{:S(2)}) %collective-permute-start.8) | collective-permute-done | bytes 90144 | tf_op jit(solution)/shard_map/ppermute | solution.py:46
  44.2 1.2 collective-permute-start.11
  45.5 1.2 collective-permute-start.14
  46.7 0.7 collective-permute-done.11.refs_9_
  47.4 1.3 %shard_map.112 = f32[208,640]{1,0:T(8,128)S(1)} custom-call(s32[16]{0:T(128)S(1)} %copy-done.5, bf16[1072,128]{1,0:T(8,128)(2,1)S(1)} %get-tuple-element.36.refs_0_, bf16[1072,128]{1,0:T(8,128)(2,1)S(1)} %collective-permute-done.refs_1_, bf16[1072,128]{1,0:T(8,128)(2,1)S(1)} %collective-permute-done.1.refs_2_, ...), custom_call_target="tpu_custom_call" | custom-call | flops 2129920 | bytes 76928 | tf_op jit(solution)/shard_map/pallas_call | solution.py:33
  48.7 1.5 %collective-permute-start.12 = (f32[208,640]{1,0:T(8,128)S(1)}, f32[208,640]{1,0:T(8,128)S(1)}, u32[]{:S(2)}, u32[]{:S(2)}) collective-permute-start(f32[208,640]{1,0:T(8,128)S(1)} %shard_map.112), channel_id=1, source_target_pairs={{16,0},{0,16},{17,1},{1,17},{18,2},{2,18},{19,3},{3,19},{20,4},{4,... | collective-permute-start | bytes 1597448 | tf_op jit(solution)/shard_map/ppermute | solution.py:46
  50.2 1.8 %collective-permute-start.13 = (bf16[1408,128]{1,0:T(8,128)(2,1)S(1)}, bf16[1408,128]{1,0:T(8,128)(2,1)S(1)}, u32[]{:S(2)}, u32[]{:S(2)}) collective-permute-start(bf16[1408,128]{1,0:T(8,128)(2,1)S(1)} %constant_dynamic-update-slice_fusion.refs_10_), channel_id=1, source_target_pairs={{1,0},{0,1},{3,2},{2,3},{5,4},{4,5},{7,6},{6,7},{9,8},{8,9},{11,10... | collective-permute-start | bytes 1081352 | tf_op jit(solution)/shard_map/ppermute | solution.py:50
  52.0 3.6 %collective-permute-done.14.refs_12_ = bf16[1408,128]{1,0:T(8,128)(2,1)S(1)} collective-permute-done((bf16[1408,128]{1,0:T(8,128)(2,1)S(1)}, bf16[1408,128]{1,0:T(8,128)(2,1)S(1)}, u32[]{:S(2)}, u32[]{:S(2)}) %collective-permute-start.14) | collective-permute-done | bytes 360480 | tf_op jit(solution)/shard_map/ppermute | solution.py:50
  55.6 0.8 collective-permute-start.15
  56.4 1.3 %shard_map.113.refs_0_ = f32[208,640]{1,0:T(8,128)S(1)} custom-call(s32[16]{0:T(128)S(1)} %copy-done.5, bf16[1072,128]{1,0:T(8,128)(2,1)S(1)} %get-tuple-element.36.refs_0_, bf16[1072,128]{1,0:T(8,128)(2,1)S(1)} %collective-permute-done.refs_1_, bf16[1072,128]{1,0:T(8,128)(2,1)S(1)} %collective-permute-done.1.refs_2_, ...), custom_call_target="tpu_custom_call" | custom-call | flops 2129920 | bytes 76928 | tf_op jit(solution)/shard_map/pallas_call | solution.py:33
  57.8 1.3 %shard_map.114 = f32[176,640]{1,0:T(8,128)S(1)} custom-call(s32[16]{0:T(128)S(1)} %copy-done.5, bf16[1072,128]{1,0:T(8,128)(2,1)S(1)} %get-tuple-element.36.refs_0_, bf16[1072,128]{1,0:T(8,128)(2,1)S(1)} %collective-permute-done.refs_1_, bf16[1072,128]{1,0:T(8,128)(2,1)S(1)} %collective-permute-done.1.refs_2_, ...), custom_call_target="tpu_custom_call" | custom-call | flops 1802240 | bytes 98176 | tf_op jit(solution)/shard_map/pallas_call | solution.py:33
  59.1 1.1 collective-permute-done.12.refs_1_
  60.7 2.2 %collective-permute-start.16 = (f32[176,640]{1,0:T(8,128)S(1)}, f32[176,640]{1,0:T(8,128)S(1)}, u32[]{:S(2)}, u32[]{:S(2)}) collective-permute-start(f32[176,640]{1,0:T(8,128)S(1)} %shard_map.114), channel_id=1, source_target_pairs={{16,0},{0,16},{17,1},{1,17},{18,2},{2,18},{19,3},{3,19},{20,4},{4,... | collective-permute-start | bytes 1351688 | tf_op jit(solution)/shard_map/ppermute | solution.py:46
  62.9 2.1 %collective-permute-start.20 = (bf16[208,640]{1,0:T(8,128)(2,1)S(1)}, bf16[208,640]{1,0:T(8,128)(2,1)S(1)}, u32[]{:S(2)}, u32[]{:S(2)}) collective-permute-start(bf16[208,640]{1,0:T(8,128)(2,1)S(1)} %get-tuple-element.48), channel_id=1, source_target_pairs={{4,0},{5,1},{6,2},{7,3},{8,4},{9,5},{10,6},{11,7},{12,8},{13,9},{1... | collective-permute-start | bytes 798728 | tf_op jit(solution)/shard_map/ppermute | solution.py:46
  64.9 1.3 %collective-permute-start.19 = (bf16[208,640]{1,0:T(8,128)(2,1)S(1)}, bf16[208,640]{1,0:T(8,128)(2,1)S(1)}, u32[]{:S(2)}, u32[]{:S(2)}) collective-permute-start(bf16[208,640]{1,0:T(8,128)(2,1)S(1)} %get-tuple-element.48), channel_id=1, source_target_pairs={{8,0},{9,1},{10,2},{11,3},{12,4},{13,5},{14,6},{15,7},{0,8},{1,9},... | collective-permute-start | bytes 798728 | tf_op jit(solution)/shard_map/ppermute | solution.py:46
  66.3 0.9 collective-permute-start.17
  67.2 1.5 %shard_map.116.refs_0_ = f32[176,640]{1,0:T(8,128)S(1)} custom-call(s32[16]{0:T(128)S(1)} %copy-done.5, bf16[1072,128]{1,0:T(8,128)(2,1)S(1)} %get-tuple-element.36.refs_0_, bf16[1072,128]{1,0:T(8,128)(2,1)S(1)} %collective-permute-done.refs_1_, bf16[1072,128]{1,0:T(8,128)(2,1)S(1)} %collective-permute-done.1.refs_2_, ...), custom_call_target="tpu_custom_call" | custom-call | flops 1802240 | bytes 98176 | tf_op jit(solution)/shard_map/pallas_call | solution.py:33
  68.7 2.1 %collective-permute-done.16.refs_1_ = f32[176,640]{1,0:T(8,128)S(1)} collective-permute-done((f32[176,640]{1,0:T(8,128)S(1)}, f32[176,640]{1,0:T(8,128)S(1)}, u32[]{:S(2)}, u32[]{:S(2)}) %collective-permute-start.16) | collective-permute-done | bytes 450592 | tf_op jit(solution)/shard_map/ppermute | solution.py:46
  70.8 1.7 %shard_map.117 = (f32[384,640]{1,0:T(8,128)}, f32[384,640]{1,0:T(8,128)}, f32[384,640]{1,0:T(8,128)}, bf16[176,640]{1,0:T(8,128)(2,1)S(1)}) custom-call(f32[176,640]{1,0:T(8,128)S(1)} %shard_map.116.refs_0_, f32[176,640]{1,0:T(8,128)S(1)} %collective-permute-done.16.refs_1_, f32[384,640]{1,0:T(8,128)S(1)} %bitcast.8, f32[384,640]{1,0:T(8,128)S(1)} %bitcast.10, ...), custom_call_target="tpu_custom_call" | custom-call | flops 112640 | bytes 112640 | tf_op jit(solution)/shard_map/pallas_call | solution.py:230
  72.5 4.1 %collective-permute-start.18 = (bf16[176,640]{1,0:T(8,128)(2,1)S(1)}, bf16[176,640]{1,0:T(8,128)(2,1)S(1)}, u32[]{:S(2)}, u32[]{:S(2)}) collective-permute-start(bf16[176,640]{1,0:T(8,128)(2,1)S(1)} %get-tuple-element.58.refs_0_), channel_id=1, source_target_pairs={{2,0},{3,1},{0,2},{1,3},{6,4},{7,5},{4,6},{5,7},{10,8},{11,9},{8,1... | collective-permute-start | bytes 675848 | tf_op jit(solution)/shard_map/ppermute | solution.py:50
  76.7 3.9 %collective-permute-done.18.refs_2_ = bf16[176,640]{1,0:T(8,128)(2,1)S(1)} collective-permute-done((bf16[176,640]{1,0:T(8,128)(2,1)S(1)}, bf16[176,640]{1,0:T(8,128)(2,1)S(1)}, u32[]{:S(2)}, u32[]{:S(2)}) %collective-permute-start.18) | collective-permute-done | bytes 225312 | tf_op jit(solution)/shard_map/ppermute | solution.py:50
  80.6 2.7 %collective-permute-done.19 = bf16[208,640]{1,0:T(8,128)(2,1)S(1)} collective-permute-done((bf16[208,640]{1,0:T(8,128)(2,1)S(1)}, bf16[208,640]{1,0:T(8,128)(2,1)S(1)}, u32[]{:S(2)}, u32[]{:S(2)}) %collective-permute-start.19) | collective-permute-done | bytes 266272 | tf_op jit(solution)/shard_map/ppermute | solution.py:46
  83.3 5.7 %collective-permute-done.17 = bf16[208,640]{1,0:T(8,128)(2,1)S(1)} collective-permute-done((bf16[208,640]{1,0:T(8,128)(2,1)S(1)}, bf16[208,640]{1,0:T(8,128)(2,1)S(1)}, u32[]{:S(2)}, u32[]{:S(2)}) %collective-permute-start.17) | collective-permute-done | bytes 266272 | tf_op jit(solution)/shard_map/ppermute | solution.py:46
  89.1 2.7 %collective-permute-start.21 = (bf16[832,640]{1,0:T(8,128)(2,1)S(1)}, bf16[832,640]{1,0:T(8,128)(2,1)S(1)}, u32[]{:S(2)}, u32[]{:S(2)}) collective-permute-start(bf16[832,640]{1,0:T(8,128)(2,1)S(1)} %constant_dynamic-update-slice_fusion.4.refs_0_), channel_id=1, source_target_pairs={{2,0},{3,1},{0,2},{1,3},{6,4},{7,5},{4,6},{5,7},{10,8},{11,9},{8,1... | collective-permute-start | bytes 3194888 | tf_op jit(solution)/shard_map/ppermute | solution.py:50
  91.8 0.8 collective-permute-start.22
  92.6 1.1 collective-permute-done.22.refs_1_
  94.1 0.7 shard_map.119
  94.8 2.3 %collective-permute-start.24 = (bf16[176,640]{1,0:T(8,128)(2,1)S(1)}, bf16[176,640]{1,0:T(8,128)(2,1)S(1)}, u32[]{:S(2)}, u32[]{:S(2)}) collective-permute-start(bf16[176,640]{1,0:T(8,128)(2,1)S(1)} %get-tuple-element.63), channel_id=1, source_target_pairs={{12,0},{13,1},{14,2},{15,3},{0,4},{1,5},{2,6},{3,7},{4,8},{5,9},{6... | collective-permute-start | bytes 675848 | tf_op jit(solution)/shard_map/ppermute | solution.py:46
  97.1 1.0 collective-permute-start.25
  98.3 16.9 %collective-permute-done.21.refs_1_ = bf16[832,640]{1,0:T(8,128)(2,1)S(1)} collective-permute-done((bf16[832,640]{1,0:T(8,128)(2,1)S(1)}, bf16[832,640]{1,0:T(8,128)(2,1)S(1)}, u32[]{:S(2)}, u32[]{:S(2)}) %collective-permute-start.21) | collective-permute-done | bytes 1064992 | tf_op jit(solution)/shard_map/ppermute | solution.py:50
  116.1 1.3 %collective-permute-done.26.refs_5_ = bf16[176,640]{1,0:T(8,128)(2,1)S(1)} collective-permute-done((bf16[176,640]{1,0:T(8,128)(2,1)S(1)}, bf16[176,640]{1,0:T(8,128)(2,1)S(1)}, u32[]{:S(2)}, u32[]{:S(2)}) %collective-permute-start.26) | collective-permute-done | bytes 225312 | tf_op jit(solution)/shard_map/ppermute | solution.py:46
  117.4 1.1 collective-permute-start.27
  118.5 1.5 %shard_map.120.refs_1_ = bf16[384,2560]{1,0:T(8,128)(2,1)} custom-call(s32[16]{0:T(128)S(1)} %copy-done.5, bf16[832,640]{1,0:T(8,128)(2,1)S(1)} %constant_dynamic-update-slice_fusion.4.refs_0_, bf16[832,640]{1,0:T(8,128)(2,1)S(1)} %collective-permute-done.21.refs_1_, bf16[176,640]{1,0:T(8,128)(2,1)S(1)} %get-tuple-element.67.refs_2_, ...), custom_call_target="tpu_custom_call" | custom-call | flops 1 | bytes 16384 | tf_op jit(solution)/shard_map/pallas_call | solution.py:320
  120.1 0.8 collective-permute-done.27.refs_0_
  120.8 1.6 %shard_map.121 = bf16[384,2560]{1,0:T(8,128)(2,1)} custom-call(s32[16]{0:T(128)S(1)} %copy-done.5, bf16[208,2560]{1,0:T(8,128)(2,1)S(1)} %collective-permute-done.27.refs_0_, bf16[384,2560]{1,0:T(8,128)(2,1)} %shard_map.120.refs_1_), custom_call_target="tpu_custom_call", output_to_operand_aliasing={{}: (2, {})} | custom-call | flops 1 | bytes 16384 | tf_op jit(solution)/shard_map/pallas_call | solution.py:320
  (42 shorter events, 3.6 us)
Async XLA Ops:
  1.9 1.1 copy-start.3
  3.0 0.9 copy-start.4
  4.1 7.5 %collective-permute-start.1 = (bf16[1072,128]{1,0:T(8,128)(2,1)S(1)}, bf16[1072,128]{1,0:T(8,128)(2,1)S(1)}, u32[]{:S(2)}, u32[]{:S(2)}) collective-permute-start(bf16[1072,128]{1,0:T(8,128)(2,1)S(1)} %get-tuple-element.37), channel_id=1, source_target_pairs={{12,0},{13,1},{14,2},{15,3},{0,4},{1,5},{2,6},{3,7},{4,8},{5,9},{6... | collective-permute-start | bytes 823304 | tf_op jit(solution)/shard_map/ppermute | solution.py:46
  5.5 13.9 %collective-permute-start.2 = (bf16[1072,128]{1,0:T(8,128)(2,1)S(1)}, bf16[1072,128]{1,0:T(8,128)(2,1)S(1)}, u32[]{:S(2)}, u32[]{:S(2)}) collective-permute-start(bf16[1072,128]{1,0:T(8,128)(2,1)S(1)} %get-tuple-element.38), channel_id=1, source_target_pairs={{4,0},{5,1},{6,2},{7,3},{8,4},{9,5},{10,6},{11,7},{12,8},{13,9},{1... | collective-permute-start | bytes 823304 | tf_op jit(solution)/shard_map/ppermute | solution.py:46
  5.6 13.8 %collective-permute-start = (bf16[1072,128]{1,0:T(8,128)(2,1)S(1)}, bf16[1072,128]{1,0:T(8,128)(2,1)S(1)}, u32[]{:S(2)}, u32[]{:S(2)}) collective-permute-start(bf16[1072,128]{1,0:T(8,128)(2,1)S(1)} %get-tuple-element.36.refs_0_), channel_id=1, source_target_pairs={{2,0},{3,1},{0,2},{1,3},{6,4},{7,5},{4,6},{5,7},{10,8},{11,9},{8,1... | collective-permute-start | bytes 823304 | tf_op jit(solution)/shard_map/ppermute | solution.py:50
  19.4 12.1 %collective-permute-start.4 = (bf16[1072,128]{1,0:T(8,128)(2,1)S(1)}, bf16[1072,128]{1,0:T(8,128)(2,1)S(1)}, u32[]{:S(2)}, u32[]{:S(2)}) collective-permute-start(bf16[1072,128]{1,0:T(8,128)(2,1)S(1)} %get-tuple-element.41), channel_id=1, source_target_pairs={{8,0},{9,1},{10,2},{11,3},{12,4},{13,5},{14,6},{15,7},{0,8},{1,9},... | collective-permute-start | bytes 823304 | tf_op jit(solution)/shard_map/ppermute | solution.py:46
  19.6 13.8 %collective-permute-start.6 = (bf16[2144,128]{1,0:T(8,128)(2,1)S(1)}, bf16[2144,128]{1,0:T(8,128)(2,1)S(1)}, u32[]{:S(2)}, u32[]{:S(2)}) collective-permute-start(bf16[2144,128]{1,0:T(8,128)(2,1)S(1)} %pad_maximum_fusion.2), channel_id=1, source_target_pairs={{2,0},{3,1},{0,2},{1,3},{6,4},{7,5},{4,6},{5,7},{10,8},{11,9},{8,1... | collective-permute-start | bytes 1646600 | tf_op jit(solution)/shard_map/ppermute | solution.py:50
  31.4 2.0 %collective-permute-start.5 = (bf16[1072,128]{1,0:T(8,128)(2,1)S(1)}, bf16[1072,128]{1,0:T(8,128)(2,1)S(1)}, u32[]{:S(2)}, u32[]{:S(2)}) collective-permute-start(bf16[1072,128]{1,0:T(8,128)(2,1)S(1)} %collective-permute-done.4.refs_5_), channel_id=1, source_target_pairs={{1,0},{0,1},{3,2},{2,3},{5,4},{4,5},{7,6},{6,7},{9,8},{8,9},{11,10... | collective-permute-start | bytes 823304 | tf_op jit(solution)/shard_map/ppermute | solution.py:50
  32.3 8.2 %collective-permute-start.7 = (bf16[1072,128]{1,0:T(8,128)(2,1)S(1)}, bf16[1072,128]{1,0:T(8,128)(2,1)S(1)}, u32[]{:S(2)}, u32[]{:S(2)}) collective-permute-start(bf16[1072,128]{1,0:T(8,128)(2,1)S(1)} %collective-permute-done.4.refs_5_), channel_id=1, source_target_pairs={{2,0},{3,1},{0,2},{1,3},{6,4},{7,5},{4,6},{5,7},{10,8},{11,9},{8,1... | collective-permute-start | bytes 823304 | tf_op jit(solution)/shard_map/ppermute | solution.py:50
  33.5 7.0 %collective-permute-start.10 = (bf16[352,128]{1,0:T(8,128)(2,1)S(1)}, bf16[352,128]{1,0:T(8,128)(2,1)S(1)}, u32[]{:S(2)}, u32[]{:S(2)}) collective-permute-start(bf16[352,128]{1,0:T(8,128)(2,1)S(1)} %get-tuple-element.43), channel_id=1, source_target_pairs={{4,0},{5,1},{6,2},{7,3},{8,4},{9,5},{10,6},{11,7},{12,8},{13,9},{1... | collective-permute-start | bytes 270344 | tf_op jit(solution)/shard_map/ppermute | solution.py:46
  36.4 4.4 %collective-permute-start.9 = (bf16[352,128]{1,0:T(8,128)(2,1)S(1)}, bf16[352,128]{1,0:T(8,128)(2,1)S(1)}, u32[]{:S(2)}, u32[]{:S(2)}) collective-permute-start(bf16[352,128]{1,0:T(8,128)(2,1)S(1)} %get-tuple-element.43), channel_id=1, source_target_pairs={{8,0},{9,1},{10,2},{11,3},{12,4},{13,5},{14,6},{15,7},{0,8},{1,9},... | collective-permute-start | bytes 270344 | tf_op jit(solution)/shard_map/ppermute | solution.py:46
  36.7 7.5 %collective-permute-start.8 = (bf16[352,128]{1,0:T(8,128)(2,1)S(1)}, bf16[352,128]{1,0:T(8,128)(2,1)S(1)}, u32[]{:S(2)}, u32[]{:S(2)}) collective-permute-start(bf16[352,128]{1,0:T(8,128)(2,1)S(1)} %get-tuple-element.43), channel_id=1, source_target_pairs={{12,0},{13,1},{14,2},{15,3},{0,4},{1,5},{2,6},{3,7},{4,8},{5,9},{6... | collective-permute-start | bytes 270344 | tf_op jit(solution)/shard_map/ppermute | solution.py:46
  39.0 8.3 %copy-start.5 = (s32[16]{0:T(128)S(1)}, s32[16]{0:T(128)}, u32[]{:S(2)}) copy-start(s32[16]{0:T(128)} %plan_ref.11) | copy-start | bytes 196
  39.0 7.6 %collective-permute-start.3 = (bf16[4288,128]{1,0:T(8,128)(2,1)S(1)}, bf16[4288,128]{1,0:T(8,128)(2,1)S(1)}, u32[]{:S(2)}, u32[]{:S(2)}) collective-permute-start(bf16[4288,128]{1,0:T(8,128)(2,1)S(1)} %pad_maximum_fusion), channel_id=1, source_target_pairs={{1,0},{0,1},{3,2},{2,3},{5,4},{4,5},{7,6},{6,7},{9,8},{8,9},{11,10... | collective-permute-start | bytes 3293192 | tf_op jit(solution)/shard_map/ppermute | solution.py:50
  44.2 3.2 %collective-permute-start.11 = (bf16[3216,128]{1,0:T(8,128)(2,1)S(1)}, bf16[3216,128]{1,0:T(8,128)(2,1)S(1)}, u32[]{:S(2)}, u32[]{:S(2)}) collective-permute-start(bf16[3216,128]{1,0:T(8,128)(2,1)S(1)} %pad_maximum_fusion.1), channel_id=1, source_target_pairs={{1,0},{0,1},{3,2},{2,3},{5,4},{4,5},{7,6},{6,7},{9,8},{8,9},{11,10... | collective-permute-start | bytes 2469896 | tf_op jit(solution)/shard_map/ppermute | solution.py:50
  45.5 10.1 %collective-permute-start.14 = (bf16[1408,128]{1,0:T(8,128)(2,1)S(1)}, bf16[1408,128]{1,0:T(8,128)(2,1)S(1)}, u32[]{:S(2)}, u32[]{:S(2)}) collective-permute-start(bf16[1408,128]{1,0:T(8,128)(2,1)S(1)} %constant_dynamic-update-slice_fusion.refs_10_), channel_id=1, source_target_pairs={{2,0},{3,1},{0,2},{1,3},{6,4},{7,5},{4,6},{5,7},{10,8},{11,9},{8,1... | collective-permute-start | bytes 1081352 | tf_op jit(solution)/shard_map/ppermute | solution.py:50
  48.7 11.5 %collective-permute-start.12 = (f32[208,640]{1,0:T(8,128)S(1)}, f32[208,640]{1,0:T(8,128)S(1)}, u32[]{:S(2)}, u32[]{:S(2)}) collective-permute-start(f32[208,640]{1,0:T(8,128)S(1)} %shard_map.112), channel_id=1, source_target_pairs={{16,0},{0,16},{17,1},{1,17},{18,2},{2,18},{19,3},{3,19},{20,4},{4,... | collective-permute-start | bytes 1597448 | tf_op jit(solution)/shard_map/ppermute | solution.py:46
  50.2 7.5 %collective-permute-start.13 = (bf16[1408,128]{1,0:T(8,128)(2,1)S(1)}, bf16[1408,128]{1,0:T(8,128)(2,1)S(1)}, u32[]{:S(2)}, u32[]{:S(2)}) collective-permute-start(bf16[1408,128]{1,0:T(8,128)(2,1)S(1)} %constant_dynamic-update-slice_fusion.refs_10_), channel_id=1, source_target_pairs={{1,0},{0,1},{3,2},{2,3},{5,4},{4,5},{7,6},{6,7},{9,8},{8,9},{11,10... | collective-permute-start | bytes 1081352 | tf_op jit(solution)/shard_map/ppermute | solution.py:50
  55.6 2.2 %collective-permute-start.15 = (bf16[1408,128]{1,0:T(8,128)(2,1)S(1)}, bf16[1408,128]{1,0:T(8,128)(2,1)S(1)}, u32[]{:S(2)}, u32[]{:S(2)}) collective-permute-start(bf16[1408,128]{1,0:T(8,128)(2,1)S(1)} %collective-permute-done.14.refs_12_), channel_id=1, source_target_pairs={{1,0},{0,1},{3,2},{2,3},{5,4},{4,5},{7,6},{6,7},{9,8},{8,9},{11,10... | collective-permute-start | bytes 1081352 | tf_op jit(solution)/shard_map/ppermute | solution.py:50
  57.7 2.5 %copy-start = (f32[1,384,640]{2,1,0:T(8,128)S(1)}, f32[1,384,640]{2,1,0:T(8,128)}, u32[]{:S(2)}) copy-start(f32[1,384,640]{2,1,0:T(8,128)} %param.13) | copy-start | bytes 2949124
  57.7 2.5 %copy-start.1 = (f32[1,384,640]{2,1,0:T(8,128)S(1)}, f32[1,384,640]{2,1,0:T(8,128)}, u32[]{:S(2)}) copy-start(f32[1,384,640]{2,1,0:T(8,128)} %param.14) | copy-start | bytes 2949124
  57.7 2.5 %copy-start.2 = (f32[1,384,640]{2,1,0:T(8,128)S(1)}, f32[1,384,640]{2,1,0:T(8,128)}, u32[]{:S(2)}) copy-start(f32[1,384,640]{2,1,0:T(8,128)} %param.15) | copy-start | bytes 2949124
  60.7 10.1 %collective-permute-start.16 = (f32[176,640]{1,0:T(8,128)S(1)}, f32[176,640]{1,0:T(8,128)S(1)}, u32[]{:S(2)}, u32[]{:S(2)}) collective-permute-start(f32[176,640]{1,0:T(8,128)S(1)} %shard_map.114), channel_id=1, source_target_pairs={{16,0},{0,16},{17,1},{1,17},{18,2},{2,18},{19,3},{3,19},{20,4},{4,... | collective-permute-start | bytes 1351688 | tf_op jit(solution)/shard_map/ppermute | solution.py:46
  62.9 13.8 %collective-permute-start.20 = (bf16[208,640]{1,0:T(8,128)(2,1)S(1)}, bf16[208,640]{1,0:T(8,128)(2,1)S(1)}, u32[]{:S(2)}, u32[]{:S(2)}) collective-permute-start(bf16[208,640]{1,0:T(8,128)(2,1)S(1)} %get-tuple-element.48), channel_id=1, source_target_pairs={{4,0},{5,1},{6,2},{7,3},{8,4},{9,5},{10,6},{11,7},{12,8},{13,9},{1... | collective-permute-start | bytes 798728 | tf_op jit(solution)/shard_map/ppermute | solution.py:46
  64.9 18.4 %collective-permute-start.19 = (bf16[208,640]{1,0:T(8,128)(2,1)S(1)}, bf16[208,640]{1,0:T(8,128)(2,1)S(1)}, u32[]{:S(2)}, u32[]{:S(2)}) collective-permute-start(bf16[208,640]{1,0:T(8,128)(2,1)S(1)} %get-tuple-element.48), channel_id=1, source_target_pairs={{8,0},{9,1},{10,2},{11,3},{12,4},{13,5},{14,6},{15,7},{0,8},{1,9},... | collective-permute-start | bytes 798728 | tf_op jit(solution)/shard_map/ppermute | solution.py:46
  66.3 22.7 %collective-permute-start.17 = (bf16[208,640]{1,0:T(8,128)(2,1)S(1)}, bf16[208,640]{1,0:T(8,128)(2,1)S(1)}, u32[]{:S(2)}, u32[]{:S(2)}) collective-permute-start(bf16[208,640]{1,0:T(8,128)(2,1)S(1)} %get-tuple-element.48), channel_id=1, source_target_pairs={{12,0},{13,1},{14,2},{15,3},{0,4},{1,5},{2,6},{3,7},{4,8},{5,9},{6... | collective-permute-start | bytes 798728 | tf_op jit(solution)/shard_map/ppermute | solution.py:46
  72.5 8.1 %collective-permute-start.18 = (bf16[176,640]{1,0:T(8,128)(2,1)S(1)}, bf16[176,640]{1,0:T(8,128)(2,1)S(1)}, u32[]{:S(2)}, u32[]{:S(2)}) collective-permute-start(bf16[176,640]{1,0:T(8,128)(2,1)S(1)} %get-tuple-element.58.refs_0_), channel_id=1, source_target_pairs={{2,0},{3,1},{0,2},{1,3},{6,4},{7,5},{4,6},{5,7},{10,8},{11,9},{8,1... | collective-permute-start | bytes 675848 | tf_op jit(solution)/shard_map/ppermute | solution.py:50
  89.1 26.2 %collective-permute-start.21 = (bf16[832,640]{1,0:T(8,128)(2,1)S(1)}, bf16[832,640]{1,0:T(8,128)(2,1)S(1)}, u32[]{:S(2)}, u32[]{:S(2)}) collective-permute-start(bf16[832,640]{1,0:T(8,128)(2,1)S(1)} %constant_dynamic-update-slice_fusion.4.refs_0_), channel_id=1, source_target_pairs={{2,0},{3,1},{0,2},{1,3},{6,4},{7,5},{4,6},{5,7},{10,8},{11,9},{8,1... | collective-permute-start | bytes 3194888 | tf_op jit(solution)/shard_map/ppermute | solution.py:50
  91.8 1.9 %collective-permute-start.22 = (bf16[176,640]{1,0:T(8,128)(2,1)S(1)}, bf16[176,640]{1,0:T(8,128)(2,1)S(1)}, u32[]{:S(2)}, u32[]{:S(2)}) collective-permute-start(bf16[176,640]{1,0:T(8,128)(2,1)S(1)} %get-tuple-element.58.refs_0_), channel_id=1, source_target_pairs={{1,0},{0,1},{3,2},{2,3},{5,4},{4,5},{7,6},{6,7},{9,8},{8,9},{11,10... | collective-permute-start | bytes 675848 | tf_op jit(solution)/shard_map/ppermute | solution.py:50
  92.6 1.5 %collective-permute-start.23 = (bf16[176,640]{1,0:T(8,128)(2,1)S(1)}, bf16[176,640]{1,0:T(8,128)(2,1)S(1)}, u32[]{:S(2)}, u32[]{:S(2)}) collective-permute-start(bf16[176,640]{1,0:T(8,128)(2,1)S(1)} %collective-permute-done.18.refs_2_), channel_id=1, source_target_pairs={{1,0},{0,1},{3,2},{2,3},{5,4},{4,5},{7,6},{6,7},{9,8},{8,9},{11,10... | collective-permute-start | bytes 675848 | tf_op jit(solution)/shard_map/ppermute | solution.py:50
  94.8 21.2 %collective-permute-start.24 = (bf16[176,640]{1,0:T(8,128)(2,1)S(1)}, bf16[176,640]{1,0:T(8,128)(2,1)S(1)}, u32[]{:S(2)}, u32[]{:S(2)}) collective-permute-start(bf16[176,640]{1,0:T(8,128)(2,1)S(1)} %get-tuple-element.63), channel_id=1, source_target_pairs={{12,0},{13,1},{14,2},{15,3},{0,4},{1,5},{2,6},{3,7},{4,8},{5,9},{6... | collective-permute-start | bytes 675848 | tf_op jit(solution)/shard_map/ppermute | solution.py:46
  97.1 19.1 %collective-permute-start.25 = (bf16[176,640]{1,0:T(8,128)(2,1)S(1)}, bf16[176,640]{1,0:T(8,128)(2,1)S(1)}, u32[]{:S(2)}, u32[]{:S(2)}) collective-permute-start(bf16[176,640]{1,0:T(8,128)(2,1)S(1)} %get-tuple-element.64), channel_id=1, source_target_pairs={{8,0},{9,1},{10,2},{11,3},{12,4},{13,5},{14,6},{15,7},{0,8},{1,9},... | collective-permute-start | bytes 675848 | tf_op jit(solution)/shard_map/ppermute | solution.py:46
  98.1 19.3 %collective-permute-start.26 = (bf16[176,640]{1,0:T(8,128)(2,1)S(1)}, bf16[176,640]{1,0:T(8,128)(2,1)S(1)}, u32[]{:S(2)}, u32[]{:S(2)}) collective-permute-start(bf16[176,640]{1,0:T(8,128)(2,1)S(1)} %get-tuple-element.65), channel_id=1, source_target_pairs={{4,0},{5,1},{6,2},{7,3},{8,4},{9,5},{10,6},{11,7},{12,8},{13,9},{1... | collective-permute-start | bytes 675848 | tf_op jit(solution)/shard_map/ppermute | solution.py:46
  117.4 3.4 %collective-permute-start.27 = (bf16[208,2560]{1,0:T(8,128)(2,1)S(1)}, bf16[208,2560]{1,0:T(8,128)(2,1)S(1)}, u32[]{:S(2)}, u32[]{:S(2)}) collective-permute-start(bf16[208,2560]{1,0:T(8,128)(2,1)S(1)} %shard_map.118), channel_id=1, source_target_pairs={{1,0},{0,1},{3,2},{2,3},{5,4},{4,5},{7,6},{6,7},{9,8},{8,9},{11,10... | collective-permute-start | bytes 3194888 | tf_op jit(solution)/shard_map/ppermute | solution.py:50
where the time goes:
time: 123 us
  waiting for transfers between devices  67.4 us (55%)
  starting transfers between devices  38.2 us (31%)
  Pallas kernels  12.3 us (10%)
  between operations  2.3 us (2%)
  local copies, waits for them, and re-layouts  2.21 us (2%)
    ppermute x14, waiting for transfers between devices, from_behind(): return lax.ppermute(block, axis, route)  39.9 us
    ppermute x14, waiting for transfers between devices, from_mate(): lax.ppermute(block, axis, [(i ^ bit, i) for i in range(lax.axis_size(axis...  27.6 us
    ppermute x14, starting transfers between devices, from_mate(): lax.ppermute(block, axis, [(i ^ bit, i) for i in range(lax.axis_size(axis...  19.5 us
    ppermute x14, starting transfers between devices, from_behind(): return lax.ppermute(block, axis, route)  18.8 us
    pallas_call x7, Pallas kernels, call(): pl.pallas_call(kernel, out_shape=tuple(out_shapes), in_specs=[SMEM] * len...  6.96 us
    pallas_call x2, Pallas kernels, assemble(): pl.pallas_call(functools.partial(assemble_kernel, owner_count, span, late...  3.14 us
  transfers between devices with their start and end apart: 28, of which 19 were waited for; matrix products, arithmetic and copies ran while one was open for 0% of the time, Pallas kernels for 8%

commit v1 on v0

--- a/solution.py
+++ b/solution.py
@@ -243,16 +243,16 @@
     )(*terms, *states, *made)
 
 
-def choose_kernel(owner_count, plan_ref, *refs):
-    candidates, chosen = refs[:owner_count], refs[owner_count:]
+def choose_kernel(owner_count, where, plan_ref, *refs):
+    candidates, chosen = refs[: len(where)], refs[len(where) :]
     own_block, own_expert = place(owner_count)
     for step, out in enumerate(chosen):
         wanted = plan_ref[lax.rem(own_block + step, QUART) * owner_count + own_expert]
-        for mate, candidate in enumerate(candidates):
+        for (mate, rows), candidate in zip(where, candidates):
 
             @pl.when(wanted == own_expert ^ mate)
             def _():
-                out[...] = candidate[...]
+                out[rows, :] = candidate[...]
 
 
 def offer_kernel(owner_count, plan_ref, *refs):
@@ -339,7 +339,7 @@
     share_rows = hidden_units // groups
     assert block_slot.shape[1] == 1 and tok_rows == LANES and block_width % LANES == 0
     shape = jax.ShapeDtypeStruct
-    lead = share_rows * 13 // 24 // 16 * 16
+    lead = share_rows * 11 // 24 // 16 * 16
     spans = ((0, lead), (lead, share_rows - lead))
 
     head_rows = (block_width // LANES) * tok_rows + META_ROWS
@@ -425,13 +425,28 @@
     came_two = [after(term, fresh_one) for term in came_two]
     *held, fresh_two = update((*near_two, *came_two), states, spans[1], made)
 
-    mates_two = gather_mates(fresh_two, "expert", owner_count)
-    lines[1:] = [after(line, mates_two[owner_count // 2]) for line in lines[1:]]
+    rows_two = spans[1][1]
+    cut = rows_two // 32 * 16
+    halves = [(slice(0, cut), fresh_two[:cut]), (slice(cut, rows_two), fresh_two[cut:])]
+    mates_two = {0: [(slice(0, rows_two), fresh_two)]}
+    for bit in (first_bit, *other_bits):
+        mates_two.update(
+            {
+                m | bit: [
+                    (rows, from_mate(piece, "expert", bit))
+                    for rows, piece in (halves if bit == first_bit else pieces)
+                ]
+                for m, pieces in list(mates_two.items())
+            }
+        )
+    crossed_two = [piece for _, piece in mates_two[first_bit]]
+    where = [(m, rows) for m, pieces in mates_two.items() for rows, _ in pieces]
+    lines[1:] = [after(line, *crossed_two) for line in lines[1:]]
     chosen = call(
-        functools.partial(choose_kernel, owner_count),
-        [block(spans[1][1])] * QUART,
+        functools.partial(choose_kernel, owner_count, where),
+        [block(rows_two)] * QUART,
         (after(replica_plan, *lines),),
-        mates_two,
+        [piece for pieces in mates_two.values() for _, piece in pieces],
     )
     received = [across(c, step) for step, c in enumerate(chosen)]
 

time: 123 us -> 121 us (0.984)
  starting transfers between devices: 38.2 us -> 32.8 us
  waiting for transfers between devices: 67.4 us -> 69.5 us
    ppermute x14, waiting for transfers between devices: 39.9 us -> 44.1 us  [from_behind(): return lax.ppermute(block, axis, route)]
    ppermute x14 -> x16, starting transfers between devices: 19.5 us -> 15.4 us  [from_mate(): lax.ppermute(block, axis, [(i ^ bit, i) for i in range(lax.axis_size(axis...]
    ppermute x14 -> x16, waiting for transfers between devices: 27.6 us -> 25.4 us  [from_mate(): lax.ppermute(block, axis, [(i ^ bit, i) for i in range(lax.axis_size(axis...]
    ppermute x14, starting transfers between devices: 18.8 us -> 17.4 us  [from_behind(): return lax.ppermute(block, axis, route)]
  transfers between devices with their start and end apart: 28 -> 30, of which waited for: 19 -> 15; matrix products, arithmetic and copies ran while one was open for 0% -> 0% of each run, Pallas kernels for 8% -> 9%
where the time goes in v1:
time: 121 us; the launch traced here: 120 us
  waiting for transfers between devices  69.5 us (57%)
  starting transfers between devices  32.8 us (27%)
  Pallas kernels  13 us (11%)
  local copies, waits for them, and re-layouts  2.39 us (2%)
  between operations  2.34 us (2%)
    ppermute x14, waiting for transfers between devices, from_behind(): return lax.ppermute(block, axis, route)  44.1 us
    ppermute x16, waiting for transfers between devices, from_mate(): lax.ppermute(block, axis, [(i ^ bit, i) for i in range(lax.axis_size(axis...  25.4 us
    ppermute x14, starting transfers between devices, from_behind(): return lax.ppermute(block, axis, route)  17.4 us
    ppermute x16, starting transfers between devices, from_mate(): lax.ppermute(block, axis, [(i ^ bit, i) for i in range(lax.axis_size(axis...  15.4 us
    pallas_call x7, Pallas kernels, call(): pl.pallas_call(kernel, out_shape=tuple(out_shapes), in_specs=[SMEM] * len...  7.78 us
    pallas_call x2, Pallas kernels, assemble(): pl.pallas_call(functools.partial(assemble_kernel, owner_count, span, late...  3.14 us
  transfers between devices with their start and end apart: 30, of which 15 were waited for; matrix products, arithmetic and copies ran while one was open for 0% of the time, Pallas kernels for 9%

profile of v1, /device:TPU:9, one launch (start us, length us, event | category | flops | bytes accessed | tf_op | source)
XLA Modules:
  0.0 120.2 jit_solution(10225771443772951579)
XLA Ops:
  1.9 1.1 copy-done.3
  3.0 0.9 copy-done.4
  4.1 1.3 %collective-permute-start.1 = (bf16[1008,128]{1,0:T(8,128)(2,1)S(1)}, bf16[1008,128]{1,0:T(8,128)(2,1)S(1)}, u32[]{:S(2)}, u32[]{:S(2)}) collective-permute-start(bf16[1008,128]{1,0:T(8,128)(2,1)S(1)} %get-tuple-element.37), channel_id=1, source_target_pairs={{12,0},{13,1},{14,2},{15,3},{0,4},{1,5},{2,6},{3,7},{4,8},{5,9},{6... | collective-permute-start | bytes 774152 | tf_op jit(solution)/shard_map/ppermute | solution.py:46
  5.6 1.2 %collective-permute-start = (bf16[1008,128]{1,0:T(8,128)(2,1)S(1)}, bf16[1008,128]{1,0:T(8,128)(2,1)S(1)}, u32[]{:S(2)}, u32[]{:S(2)}) collective-permute-start(bf16[1008,128]{1,0:T(8,128)(2,1)S(1)} %get-tuple-element.36.refs_0_), channel_id=1, source_target_pairs={{2,0},{3,1},{0,2},{1,3},{6,4},{7,5},{4,6},{5,7},{10,8},{11,9},{8,1... | collective-permute-start | bytes 774152 | tf_op jit(solution)/shard_map/ppermute | solution.py:50
  6.8 4.4 %collective-permute-done.1.refs_2_ = bf16[1008,128]{1,0:T(8,128)(2,1)S(1)} collective-permute-done((bf16[1008,128]{1,0:T(8,128)(2,1)S(1)}, bf16[1008,128]{1,0:T(8,128)(2,1)S(1)}, u32[]{:S(2)}, u32[]{:S(2)}) %collective-permute-start.1) | collective-permute-done | bytes 258080 | tf_op jit(solution)/shard_map/ppermute | solution.py:46
  11.2 7.4 %collective-permute-done.2.refs_3_ = bf16[1008,128]{1,0:T(8,128)(2,1)S(1)} collective-permute-done((bf16[1008,128]{1,0:T(8,128)(2,1)S(1)}, bf16[1008,128]{1,0:T(8,128)(2,1)S(1)}, u32[]{:S(2)}, u32[]{:S(2)}) %collective-permute-start.2) | collective-permute-done | bytes 258080 | tf_op jit(solution)/shard_map/ppermute | solution.py:46
  18.9 1.3 %collective-permute-start.6 = (bf16[2016,128]{1,0:T(8,128)(2,1)S(1)}, bf16[2016,128]{1,0:T(8,128)(2,1)S(1)}, u32[]{:S(2)}, u32[]{:S(2)}) collective-permute-start(bf16[2016,128]{1,0:T(8,128)(2,1)S(1)} %pad_maximum_fusion.2), channel_id=1, source_target_pairs={{2,0},{3,1},{0,2},{1,3},{6,4},{7,5},{4,6},{5,7},{10,8},{11,9},{8,1... | collective-permute-start | bytes 1548296 | tf_op jit(solution)/shard_map/ppermute | solution.py:50
  20.2 9.8 %collective-permute-done.4.refs_5_ = bf16[1008,128]{1,0:T(8,128)(2,1)S(1)} collective-permute-done((bf16[1008,128]{1,0:T(8,128)(2,1)S(1)}, bf16[1008,128]{1,0:T(8,128)(2,1)S(1)}, u32[]{:S(2)}, u32[]{:S(2)}) %collective-permute-start.4) | collective-permute-done | bytes 258080 | tf_op jit(solution)/shard_map/ppermute | solution.py:46
  30.0 0.8 collective-permute-start.5
  30.9 1.2 %collective-permute-start.7 = (bf16[1008,128]{1,0:T(8,128)(2,1)S(1)}, bf16[1008,128]{1,0:T(8,128)(2,1)S(1)}, u32[]{:S(2)}, u32[]{:S(2)}) collective-permute-start(bf16[1008,128]{1,0:T(8,128)(2,1)S(1)} %collective-permute-done.4.refs_5_), channel_id=1, source_target_pairs={{2,0},{3,1},{0,2},{1,3},{6,4},{7,5},{4,6},{5,7},{10,8},{11,9},{8,1... | collective-permute-start | bytes 774152 | tf_op jit(solution)/shard_map/ppermute | solution.py:50
  32.1 2.9 %collective-permute-start.10 = (bf16[416,128]{1,0:T(8,128)(2,1)S(1)}, bf16[416,128]{1,0:T(8,128)(2,1)S(1)}, u32[]{:S(2)}, u32[]{:S(2)}) collective-permute-start(bf16[416,128]{1,0:T(8,128)(2,1)S(1)} %get-tuple-element.43), channel_id=1, source_target_pairs={{4,0},{5,1},{6,2},{7,3},{8,4},{9,5},{10,6},{11,7},{12,8},{13,9},{1... | collective-permute-start | bytes 319496 | tf_op jit(solution)/shard_map/ppermute | solution.py:46
  35.3 2.3 %collective-permute-start.8 = (bf16[416,128]{1,0:T(8,128)(2,1)S(1)}, bf16[416,128]{1,0:T(8,128)(2,1)S(1)}, u32[]{:S(2)}, u32[]{:S(2)}) collective-permute-start(bf16[416,128]{1,0:T(8,128)(2,1)S(1)} %get-tuple-element.43), channel_id=1, source_target_pairs={{12,0},{13,1},{14,2},{15,3},{0,4},{1,5},{2,6},{3,7},{4,8},{5,9},{6... | collective-permute-start | bytes 319496 | tf_op jit(solution)/shard_map/ppermute | solution.py:46
  37.7 1.2 collective-permute-start.3
  38.9 2.6 %collective-permute-done.9 = bf16[416,128]{1,0:T(8,128)(2,1)S(1)} collective-permute-done((bf16[416,128]{1,0:T(8,128)(2,1)S(1)}, bf16[416,128]{1,0:T(8,128)(2,1)S(1)}, u32[]{:S(2)}, u32[]{:S(2)}) %collective-permute-start.9) | collective-permute-done | bytes 106528 | tf_op jit(solution)/shard_map/ppermute | solution.py:46
  41.5 2.8 %collective-permute-done.8 = bf16[416,128]{1,0:T(8,128)(2,1)S(1)} collective-permute-done((bf16[416,128]{1,0:T(8,128)(2,1)S(1)}, bf16[416,128]{1,0:T(8,128)(2,1)S(1)}, u32[]{:S(2)}, u32[]{:S(2)}) %collective-permute-start.8) | collective-permute-done | bytes 106528 | tf_op jit(solution)/shard_map/ppermute | solution.py:46
  44.3 1.2 collective-permute-start.11
  45.6 1.1 collective-permute-start.14
  46.7 0.7 collective-permute-done.11.refs_9_
  47.4 1.5 %shard_map.112 = f32[176,640]{1,0:T(8,128)S(1)} custom-call(s32[16]{0:T(128)S(1)} %copy-done.5, bf16[1008,128]{1,0:T(8,128)(2,1)S(1)} %get-tuple-element.36.refs_0_, bf16[1008,128]{1,0:T(8,128)(2,1)S(1)} %collective-permute-done.refs_1_, bf16[1008,128]{1,0:T(8,128)(2,1)S(1)} %collective-permute-done.1.refs_2_, ...), custom_call_target="tpu_custom_call" | custom-call | flops 1802240 | bytes 71552 | tf_op jit(solution)/shard_map/pallas_call | solution.py:33
  48.9 1.3 %collective-permute-start.12 = (f32[176,640]{1,0:T(8,128)S(1)}, f32[176,640]{1,0:T(8,128)S(1)}, u32[]{:S(2)}, u32[]{:S(2)}) collective-permute-start(f32[176,640]{1,0:T(8,128)S(1)} %shard_map.112), channel_id=1, source_target_pairs={{16,0},{0,16},{17,1},{1,17},{18,2},{2,18},{19,3},{3,19},{20,4},{4,... | collective-permute-start | bytes 1351688 | tf_op jit(solution)/shard_map/ppermute | solution.py:46
  50.2 1.5 %collective-permute-start.13 = (bf16[1664,128]{1,0:T(8,128)(2,1)S(1)}, bf16[1664,128]{1,0:T(8,128)(2,1)S(1)}, u32[]{:S(2)}, u32[]{:S(2)}) collective-permute-start(bf16[1664,128]{1,0:T(8,128)(2,1)S(1)} %constant_dynamic-update-slice_fusion.refs_10_), channel_id=1, source_target_pairs={{1,0},{0,1},{3,2},{2,3},{5,4},{4,5},{7,6},{6,7},{9,8},{8,9},{11,10... | collective-permute-start | bytes 1277960 | tf_op jit(solution)/shard_map/ppermute | solution.py:50
  51.7 5.4 %collective-permute-done.14.refs_12_ = bf16[1664,128]{1,0:T(8,128)(2,1)S(1)} collective-permute-done((bf16[1664,128]{1,0:T(8,128)(2,1)S(1)}, bf16[1664,128]{1,0:T(8,128)(2,1)S(1)}, u32[]{:S(2)}, u32[]{:S(2)}) %collective-permute-start.14) | collective-permute-done | bytes 426016 | tf_op jit(solution)/shard_map/ppermute | solution.py:50
  57.0 0.8 collective-permute-start.15
  57.8 1.5 %shard_map.113.refs_0_ = f32[176,640]{1,0:T(8,128)S(1)} custom-call(s32[16]{0:T(128)S(1)} %copy-done.5, bf16[1008,128]{1,0:T(8,128)(2,1)S(1)} %get-tuple-element.36.refs_0_, bf16[1008,128]{1,0:T(8,128)(2,1)S(1)} %collective-permute-done.refs_1_, bf16[1008,128]{1,0:T(8,128)(2,1)S(1)} %collective-permute-done.1.refs_2_, ...), custom_call_target="tpu_custom_call" | custom-call | flops 1802240 | bytes 71552 | tf_op jit(solution)/shard_map/pallas_call | solution.py:33
  59.4 1.5 %shard_map.114 = f32[208,640]{1,0:T(8,128)S(1)} custom-call(s32[16]{0:T(128)S(1)} %copy-done.5, bf16[1008,128]{1,0:T(8,128)(2,1)S(1)} %get-tuple-element.36.refs_0_, bf16[1008,128]{1,0:T(8,128)(2,1)S(1)} %collective-permute-done.refs_1_, bf16[1008,128]{1,0:T(8,128)(2,1)S(1)} %collective-permute-done.1.refs_2_, ...), custom_call_target="tpu_custom_call" | custom-call | flops 2129920 | bytes 99456 | tf_op jit(solution)/shard_map/pallas_call | solution.py:33
  61.6 1.3 %collective-permute-start.16 = (f32[208,640]{1,0:T(8,128)S(1)}, f32[208,640]{1,0:T(8,128)S(1)}, u32[]{:S(2)}, u32[]{:S(2)}) collective-permute-start(f32[208,640]{1,0:T(8,128)S(1)} %shard_map.114), channel_id=1, source_target_pairs={{16,0},{0,16},{17,1},{1,17},{18,2},{2,18},{19,3},{3,19},{20,4},{4,... | collective-permute-start | bytes 1597448 | tf_op jit(solution)/shard_map/ppermute | solution.py:46
  62.9 1.9 %collective-permute-start.21 = (bf16[176,640]{1,0:T(8,128)(2,1)S(1)}, bf16[176,640]{1,0:T(8,128)(2,1)S(1)}, u32[]{:S(2)}, u32[]{:S(2)}) collective-permute-start(bf16[176,640]{1,0:T(8,128)(2,1)S(1)} %get-tuple-element.48), channel_id=1, source_target_pairs={{4,0},{5,1},{6,2},{7,3},{8,4},{9,5},{10,6},{11,7},{12,8},{13,9},{1... | collective-permute-start | bytes 675848 | tf_op jit(solution)/shard_map/ppermute | solution.py:46
  64.7 1.5 %collective-permute-start.20 = (bf16[176,640]{1,0:T(8,128)(2,1)S(1)}, bf16[176,640]{1,0:T(8,128)(2,1)S(1)}, u32[]{:S(2)}, u32[]{:S(2)}) collective-permute-start(bf16[176,640]{1,0:T(8,128)(2,1)S(1)} %get-tuple-element.48), channel_id=1, source_target_pairs={{8,0},{9,1},{10,2},{11,3},{12,4},{13,5},{14,6},{15,7},{0,8},{1,9},... | collective-permute-start | bytes 675848 | tf_op jit(solution)/shard_map/ppermute | solution.py:46
  66.8 1.7 %shard_map.116.refs_0_ = f32[208,640]{1,0:T(8,128)S(1)} custom-call(s32[16]{0:T(128)S(1)} %copy-done.5, bf16[1008,128]{1,0:T(8,128)(2,1)S(1)} %get-tuple-element.36.refs_0_, bf16[1008,128]{1,0:T(8,128)(2,1)S(1)} %collective-permute-done.refs_1_, bf16[1008,128]{1,0:T(8,128)(2,1)S(1)} %collective-permute-done.1.refs_2_, ...), custom_call_target="tpu_custom_call" | custom-call | flops 2129920 | bytes 99456 | tf_op jit(solution)/shard_map/pallas_call | solution.py:33
  68.5 5.7 %collective-permute-done.16.refs_1_ = f32[208,640]{1,0:T(8,128)S(1)} collective-permute-done((f32[208,640]{1,0:T(8,128)S(1)}, f32[208,640]{1,0:T(8,128)S(1)}, u32[]{:S(2)}, u32[]{:S(2)}) %collective-permute-start.16) | collective-permute-done | bytes 532512 | tf_op jit(solution)/shard_map/ppermute | solution.py:46
  74.1 1.7 %shard_map.117 = (f32[384,640]{1,0:T(8,128)}, f32[384,640]{1,0:T(8,128)}, f32[384,640]{1,0:T(8,128)}, bf16[208,640]{1,0:T(8,128)(2,1)S(1)}) custom-call(f32[208,640]{1,0:T(8,128)S(1)} %shard_map.116.refs_0_, f32[208,640]{1,0:T(8,128)S(1)} %collective-permute-done.16.refs_1_, f32[384,640]{1,0:T(8,128)S(1)} %bitcast.8, f32[384,640]{1,0:T(8,128)S(1)} %bitcast.10, ...), custom_call_target="tpu_custom_call" | custom-call | flops 133120 | bytes 133120 | tf_op jit(solution)/shard_map/pallas_call | solution.py:230
  76.1 1.4 %collective-permute-start.18 = (bf16[96,640]{1,0:T(8,128)(2,1)S(1)}, bf16[96,640]{1,0:T(8,128)(2,1)S(1)}, u32[]{:S(2)}, u32[]{:S(2)}) collective-permute-start(bf16[96,640]{1,0:T(8,128)(2,1)S(1)} %slice.6), channel_id=1, source_target_pairs={{2,0},{3,1},{0,2},{1,3},{6,4},{7,5},{4,6},{5,7},{10,8},{11,9},{8,1... | collective-permute-start | bytes 368648 | tf_op jit(solution)/shard_map/ppermute | solution.py:50
  77.5 4.3 %collective-permute-done.18.refs_1_ = bf16[96,640]{1,0:T(8,128)(2,1)S(1)} collective-permute-done((bf16[96,640]{1,0:T(8,128)(2,1)S(1)}, bf16[96,640]{1,0:T(8,128)(2,1)S(1)}, u32[]{:S(2)}, u32[]{:S(2)}) %collective-permute-start.18) | collective-permute-done | bytes 122912 | tf_op jit(solution)/shard_map/ppermute | solution.py:50
  81.8 3.2 %collective-permute-done.17 = bf16[176,640]{1,0:T(8,128)(2,1)S(1)} collective-permute-done((bf16[176,640]{1,0:T(8,128)(2,1)S(1)}, bf16[176,640]{1,0:T(8,128)(2,1)S(1)}, u32[]{:S(2)}, u32[]{:S(2)}) %collective-permute-start.17) | collective-permute-done | bytes 225312 | tf_op jit(solution)/shard_map/ppermute | solution.py:46
  85.1 0.9 collective-permute-start.22
  86.0 0.8 collective-permute-start.23
  86.8 0.5 collective-permute-start.24
  87.3 1.0 collective-permute-done.24.refs_4_
  88.3 0.7 shard_map.119
  89.1 2.3 %collective-permute-start.26 = (bf16[208,640]{1,0:T(8,128)(2,1)S(1)}, bf16[208,640]{1,0:T(8,128)(2,1)S(1)}, u32[]{:S(2)}, u32[]{:S(2)}) collective-permute-start(bf16[208,640]{1,0:T(8,128)(2,1)S(1)} %get-tuple-element.63), channel_id=1, source_target_pairs={{12,0},{13,1},{14,2},{15,3},{0,4},{1,5},{2,6},{3,7},{4,8},{5,9},{6... | collective-permute-start | bytes 798728 | tf_op jit(solution)/shard_map/ppermute | solution.py:46
  91.3 1.4 %collective-permute-start.27 = (bf16[208,640]{1,0:T(8,128)(2,1)S(1)}, bf16[208,640]{1,0:T(8,128)(2,1)S(1)}, u32[]{:S(2)}, u32[]{:S(2)}) collective-permute-start(bf16[208,640]{1,0:T(8,128)(2,1)S(1)} %get-tuple-element.64), channel_id=1, source_target_pairs={{8,0},{9,1},{10,2},{11,3},{12,4},{13,5},{14,6},{15,7},{0,8},{1,9},... | collective-permute-start | bytes 798728 | tf_op jit(solution)/shard_map/ppermute | solution.py:46
  92.8 13.5 %collective-permute-done.22.refs_1_ = bf16[704,640]{1,0:T(8,128)(2,1)S(1)} collective-permute-done((bf16[704,640]{1,0:T(8,128)(2,1)S(1)}, bf16[704,640]{1,0:T(8,128)(2,1)S(1)}, u32[]{:S(2)}, u32[]{:S(2)}) %collective-permute-start.22) | collective-permute-done | bytes 901152 | tf_op jit(solution)/shard_map/ppermute | solution.py:50
  106.3 0.7 shard_map.118
  107.0 6.9 %collective-permute-done.27.refs_4_ = bf16[208,640]{1,0:T(8,128)(2,1)S(1)} collective-permute-done((bf16[208,640]{1,0:T(8,128)(2,1)S(1)}, bf16[208,640]{1,0:T(8,128)(2,1)S(1)}, u32[]{:S(2)}, u32[]{:S(2)}) %collective-permute-start.27) | collective-permute-done | bytes 266272 | tf_op jit(solution)/shard_map/ppermute | solution.py:46
  113.9 1.3 %collective-permute-done.28.refs_5_ = bf16[208,640]{1,0:T(8,128)(2,1)S(1)} collective-permute-done((bf16[208,640]{1,0:T(8,128)(2,1)S(1)}, bf16[208,640]{1,0:T(8,128)(2,1)S(1)}, u32[]{:S(2)}, u32[]{:S(2)}) %collective-permute-start.28) | collective-permute-done | bytes 266272 | tf_op jit(solution)/shard_map/ppermute | solution.py:46
  115.1 1.3 %collective-permute-start.29 = (bf16[176,2560]{1,0:T(8,128)(2,1)S(1)}, bf16[176,2560]{1,0:T(8,128)(2,1)S(1)}, u32[]{:S(2)}, u32[]{:S(2)}) collective-permute-start(bf16[176,2560]{1,0:T(8,128)(2,1)S(1)} %shard_map.118), channel_id=1, source_target_pairs={{1,0},{0,1},{3,2},{2,3},{5,4},{4,5},{7,6},{6,7},{9,8},{8,9},{11,10... | collective-permute-start | bytes 2703368 | tf_op jit(solution)/shard_map/ppermute | solution.py:50
  116.4 1.6 %shard_map.120.refs_1_ = bf16[384,2560]{1,0:T(8,128)(2,1)} custom-call(s32[16]{0:T(128)S(1)} %copy-done.5, bf16[704,640]{1,0:T(8,128)(2,1)S(1)} %constant_dynamic-update-slice_fusion.4.refs_0_, bf16[704,640]{1,0:T(8,128)(2,1)S(1)} %collective-permute-done.22.refs_1_, bf16[208,640]{1,0:T(8,128)(2,1)S(1)} %get-tuple-element.67.refs_2_, ...), custom_call_target="tpu_custom_call" | custom-call | flops 1 | bytes 16384 | tf_op jit(solution)/shard_map/pallas_call | solution.py:320
  118.5 1.5 %shard_map.121 = bf16[384,2560]{1,0:T(8,128)(2,1)} custom-call(s32[16]{0:T(128)S(1)} %copy-done.5, bf16[176,2560]{1,0:T(8,128)(2,1)S(1)} %collective-permute-done.29.refs_0_, bf16[384,2560]{1,0:T(8,128)(2,1)} %shard_map.120.refs_1_), custom_call_target="tpu_custom_call", output_to_operand_aliasing={{}: (2, {})} | custom-call | flops 1 | bytes 16384 | tf_op jit(solution)/shard_map/pallas_call | solution.py:320
  (48 shorter events, 3.0 us)
Async XLA Ops:
  1.9 1.1 copy-start.3
  3.0 0.9 copy-start.4
  4.1 7.1 %collective-permute-start.1 = (bf16[1008,128]{1,0:T(8,128)(2,1)S(1)}, bf16[1008,128]{1,0:T(8,128)(2,1)S(1)}, u32[]{:S(2)}, u32[]{:S(2)}) collective-permute-start(bf16[1008,128]{1,0:T(8,128)(2,1)S(1)} %get-tuple-element.37), channel_id=1, source_target_pairs={{12,0},{13,1},{14,2},{15,3},{0,4},{1,5},{2,6},{3,7},{4,8},{5,9},{6... | collective-permute-start | bytes 774152 | tf_op jit(solution)/shard_map/ppermute | solution.py:46
  5.4 13.2 %collective-permute-start.2 = (bf16[1008,128]{1,0:T(8,128)(2,1)S(1)}, bf16[1008,128]{1,0:T(8,128)(2,1)S(1)}, u32[]{:S(2)}, u32[]{:S(2)}) collective-permute-start(bf16[1008,128]{1,0:T(8,128)(2,1)S(1)} %get-tuple-element.38), channel_id=1, source_target_pairs={{4,0},{5,1},{6,2},{7,3},{8,4},{9,5},{10,6},{11,7},{12,8},{13,9},{1... | collective-permute-start | bytes 774152 | tf_op jit(solution)/shard_map/ppermute | solution.py:46
  5.6 13.1 %collective-permute-start = (bf16[1008,128]{1,0:T(8,128)(2,1)S(1)}, bf16[1008,128]{1,0:T(8,128)(2,1)S(1)}, u32[]{:S(2)}, u32[]{:S(2)}) collective-permute-start(bf16[1008,128]{1,0:T(8,128)(2,1)S(1)} %get-tuple-element.36.refs_0_), channel_id=1, source_target_pairs={{2,0},{3,1},{0,2},{1,3},{6,4},{7,5},{4,6},{5,7},{10,8},{11,9},{8,1... | collective-permute-start | bytes 774152 | tf_op jit(solution)/shard_map/ppermute | solution.py:50
  18.7 11.4 %collective-permute-start.4 = (bf16[1008,128]{1,0:T(8,128)(2,1)S(1)}, bf16[1008,128]{1,0:T(8,128)(2,1)S(1)}, u32[]{:S(2)}, u32[]{:S(2)}) collective-permute-start(bf16[1008,128]{1,0:T(8,128)(2,1)S(1)} %get-tuple-element.41), channel_id=1, source_target_pairs={{8,0},{9,1},{10,2},{11,3},{12,4},{13,5},{14,6},{15,7},{0,8},{1,9},... | collective-permute-start | bytes 774152 | tf_op jit(solution)/shard_map/ppermute | solution.py:46
  18.9 13.1 %collective-permute-start.6 = (bf16[2016,128]{1,0:T(8,128)(2,1)S(1)}, bf16[2016,128]{1,0:T(8,128)(2,1)S(1)}, u32[]{:S(2)}, u32[]{:S(2)}) collective-permute-start(bf16[2016,128]{1,0:T(8,128)(2,1)S(1)} %pad_maximum_fusion.2), channel_id=1, source_target_pairs={{2,0},{3,1},{0,2},{1,3},{6,4},{7,5},{4,6},{5,7},{10,8},{11,9},{8,1... | collective-permute-start | bytes 1548296 | tf_op jit(solution)/shard_map/ppermute | solution.py:50
  30.0 2.0 %collective-permute-start.5 = (bf16[1008,128]{1,0:T(8,128)(2,1)S(1)}, bf16[1008,128]{1,0:T(8,128)(2,1)S(1)}, u32[]{:S(2)}, u32[]{:S(2)}) collective-permute-start(bf16[1008,128]{1,0:T(8,128)(2,1)S(1)} %collective-permute-done.4.refs_5_), channel_id=1, source_target_pairs={{1,0},{0,1},{3,2},{2,3},{5,4},{4,5},{7,6},{6,7},{9,8},{8,9},{11,10... | collective-permute-start | bytes 774152 | tf_op jit(solution)/shard_map/ppermute | solution.py:50
  30.9 8.0 %collective-permute-start.7 = (bf16[1008,128]{1,0:T(8,128)(2,1)S(1)}, bf16[1008,128]{1,0:T(8,128)(2,1)S(1)}, u32[]{:S(2)}, u32[]{:S(2)}) collective-permute-start(bf16[1008,128]{1,0:T(8,128)(2,1)S(1)} %collective-permute-done.4.refs_5_), channel_id=1, source_target_pairs={{2,0},{3,1},{0,2},{1,3},{6,4},{7,5},{4,6},{5,7},{10,8},{11,9},{8,1... | collective-permute-start | bytes 774152 | tf_op jit(solution)/shard_map/ppermute | solution.py:50
  32.1 15.3 %copy-start.5 = (s32[16]{0:T(128)S(1)}, s32[16]{0:T(128)}, u32[]{:S(2)}) copy-start(s32[16]{0:T(128)} %plan_ref.11) | copy-start | bytes 196
  32.1 6.8 %collective-permute-start.10 = (bf16[416,128]{1,0:T(8,128)(2,1)S(1)}, bf16[416,128]{1,0:T(8,128)(2,1)S(1)}, u32[]{:S(2)}, u32[]{:S(2)}) collective-permute-start(bf16[416,128]{1,0:T(8,128)(2,1)S(1)} %get-tuple-element.43), channel_id=1, source_target_pairs={{4,0},{5,1},{6,2},{7,3},{8,4},{9,5},{10,6},{11,7},{12,8},{13,9},{1... | collective-permute-start | bytes 319496 | tf_op jit(solution)/shard_map/ppermute | solution.py:46
  35.0 6.5 %collective-permute-start.9 = (bf16[416,128]{1,0:T(8,128)(2,1)S(1)}, bf16[416,128]{1,0:T(8,128)(2,1)S(1)}, u32[]{:S(2)}, u32[]{:S(2)}) collective-permute-start(bf16[416,128]{1,0:T(8,128)(2,1)S(1)} %get-tuple-element.43), channel_id=1, source_target_pairs={{8,0},{9,1},{10,2},{11,3},{12,4},{13,5},{14,6},{15,7},{0,8},{1,9},... | collective-permute-start | bytes 319496 | tf_op jit(solution)/shard_map/ppermute | solution.py:46
  35.3 8.9 %collective-permute-start.8 = (bf16[416,128]{1,0:T(8,128)(2,1)S(1)}, bf16[416,128]{1,0:T(8,128)(2,1)S(1)}, u32[]{:S(2)}, u32[]{:S(2)}) collective-permute-start(bf16[416,128]{1,0:T(8,128)(2,1)S(1)} %get-tuple-element.43), channel_id=1, source_target_pairs={{12,0},{13,1},{14,2},{15,3},{0,4},{1,5},{2,6},{3,7},{4,8},{5,9},{6... | collective-permute-start | bytes 319496 | tf_op jit(solution)/shard_map/ppermute | solution.py:46
  37.7 9.0 %collective-permute-start.3 = (bf16[4032,128]{1,0:T(8,128)(2,1)S(1)}, bf16[4032,128]{1,0:T(8,128)(2,1)S(1)}, u32[]{:S(2)}, u32[]{:S(2)}) collective-permute-start(bf16[4032,128]{1,0:T(8,128)(2,1)S(1)} %pad_maximum_fusion), channel_id=1, source_target_pairs={{1,0},{0,1},{3,2},{2,3},{5,4},{4,5},{7,6},{6,7},{9,8},{8,9},{11,10... | collective-permute-start | bytes 3096584 | tf_op jit(solution)/shard_map/ppermute | solution.py:50
  44.3 3.1 %collective-permute-start.11 = (bf16[3024,128]{1,0:T(8,128)(2,1)S(1)}, bf16[3024,128]{1,0:T(8,128)(2,1)S(1)}, u32[]{:S(2)}, u32[]{:S(2)}) collective-permute-start(bf16[3024,128]{1,0:T(8,128)(2,1)S(1)} %pad_maximum_fusion.1), channel_id=1, source_target_pairs={{1,0},{0,1},{3,2},{2,3},{5,4},{4,5},{7,6},{6,7},{9,8},{8,9},{11,10... | collective-permute-start | bytes 2322440 | tf_op jit(solution)/shard_map/ppermute | solution.py:50
  45.6 11.5 %collective-permute-start.14 = (bf16[1664,128]{1,0:T(8,128)(2,1)S(1)}, bf16[1664,128]{1,0:T(8,128)(2,1)S(1)}, u32[]{:S(2)}, u32[]{:S(2)}) collective-permute-start(bf16[1664,128]{1,0:T(8,128)(2,1)S(1)} %constant_dynamic-update-slice_fusion.refs_10_), channel_id=1, source_target_pairs={{2,0},{3,1},{0,2},{1,3},{6,4},{7,5},{4,6},{5,7},{10,8},{11,9},{8,1... | collective-permute-start | bytes 1277960 | tf_op jit(solution)/shard_map/ppermute | solution.py:50
  48.9 12.1 %collective-permute-start.12 = (f32[176,640]{1,0:T(8,128)S(1)}, f32[176,640]{1,0:T(8,128)S(1)}, u32[]{:S(2)}, u32[]{:S(2)}) collective-permute-start(f32[176,640]{1,0:T(8,128)S(1)} %shard_map.112), channel_id=1, source_target_pairs={{16,0},{0,16},{17,1},{1,17},{18,2},{2,18},{19,3},{3,19},{20,4},{4,... | collective-permute-start | bytes 1351688 | tf_op jit(solution)/shard_map/ppermute | solution.py:46
  50.2 9.2 %collective-permute-start.13 = (bf16[1664,128]{1,0:T(8,128)(2,1)S(1)}, bf16[1664,128]{1,0:T(8,128)(2,1)S(1)}, u32[]{:S(2)}, u32[]{:S(2)}) collective-permute-start(bf16[1664,128]{1,0:T(8,128)(2,1)S(1)} %constant_dynamic-update-slice_fusion.refs_10_), channel_id=1, source_target_pairs={{1,0},{0,1},{3,2},{2,3},{5,4},{4,5},{7,6},{6,7},{9,8},{8,9},{11,10... | collective-permute-start | bytes 1277960 | tf_op jit(solution)/shard_map/ppermute | solution.py:50
  57.0 2.4 %collective-permute-start.15 = (bf16[1664,128]{1,0:T(8,128)(2,1)S(1)}, bf16[1664,128]{1,0:T(8,128)(2,1)S(1)}, u32[]{:S(2)}, u32[]{:S(2)}) collective-permute-start(bf16[1664,128]{1,0:T(8,128)(2,1)S(1)} %collective-permute-done.14.refs_12_), channel_id=1, source_target_pairs={{1,0},{0,1},{3,2},{2,3},{5,4},{4,5},{7,6},{6,7},{9,8},{8,9},{11,10... | collective-permute-start | bytes 1277960 | tf_op jit(solution)/shard_map/ppermute | solution.py:50
  59.3 1.6 %copy-start = (f32[1,384,640]{2,1,0:T(8,128)S(1)}, f32[1,384,640]{2,1,0:T(8,128)}, u32[]{:S(2)}) copy-start(f32[1,384,640]{2,1,0:T(8,128)} %param.13) | copy-start | bytes 2949124
  59.4 1.6 %copy-start.1 = (f32[1,384,640]{2,1,0:T(8,128)S(1)}, f32[1,384,640]{2,1,0:T(8,128)}, u32[]{:S(2)}) copy-start(f32[1,384,640]{2,1,0:T(8,128)} %param.14) | copy-start | bytes 2949124
  59.4 1.8 %copy-start.2 = (f32[1,384,640]{2,1,0:T(8,128)S(1)}, f32[1,384,640]{2,1,0:T(8,128)}, u32[]{:S(2)}) copy-start(f32[1,384,640]{2,1,0:T(8,128)} %param.15) | copy-start | bytes 2949124
  61.6 12.6 %collective-permute-start.16 = (f32[208,640]{1,0:T(8,128)S(1)}, f32[208,640]{1,0:T(8,128)S(1)}, u32[]{:S(2)}, u32[]{:S(2)}) collective-permute-start(f32[208,640]{1,0:T(8,128)S(1)} %shard_map.114), channel_id=1, source_target_pairs={{16,0},{0,16},{17,1},{1,17},{18,2},{2,18},{19,3},{3,19},{20,4},{4,... | collective-permute-start | bytes 1597448 | tf_op jit(solution)/shard_map/ppermute | solution.py:46
  62.9 14.7 %collective-permute-start.21 = (bf16[176,640]{1,0:T(8,128)(2,1)S(1)}, bf16[176,640]{1,0:T(8,128)(2,1)S(1)}, u32[]{:S(2)}, u32[]{:S(2)}) collective-permute-start(bf16[176,640]{1,0:T(8,128)(2,1)S(1)} %get-tuple-element.48), channel_id=1, source_target_pairs={{4,0},{5,1},{6,2},{7,3},{8,4},{9,5},{10,6},{11,7},{12,8},{13,9},{1... | collective-permute-start | bytes 675848 | tf_op jit(solution)/shard_map/ppermute | solution.py:46
  64.7 17.1 %collective-permute-start.20 = (bf16[176,640]{1,0:T(8,128)(2,1)S(1)}, bf16[176,640]{1,0:T(8,128)(2,1)S(1)}, u32[]{:S(2)}, u32[]{:S(2)}) collective-permute-start(bf16[176,640]{1,0:T(8,128)(2,1)S(1)} %get-tuple-element.48), channel_id=1, source_target_pairs={{8,0},{9,1},{10,2},{11,3},{12,4},{13,5},{14,6},{15,7},{0,8},{1,9},... | collective-permute-start | bytes 675848 | tf_op jit(solution)/shard_map/ppermute | solution.py:46
  66.3 18.8 %collective-permute-start.17 = (bf16[176,640]{1,0:T(8,128)(2,1)S(1)}, bf16[176,640]{1,0:T(8,128)(2,1)S(1)}, u32[]{:S(2)}, u32[]{:S(2)}) collective-permute-start(bf16[176,640]{1,0:T(8,128)(2,1)S(1)} %get-tuple-element.48), channel_id=1, source_target_pairs={{12,0},{13,1},{14,2},{15,3},{0,4},{1,5},{2,6},{3,7},{4,8},{5,9},{6... | collective-permute-start | bytes 675848 | tf_op jit(solution)/shard_map/ppermute | solution.py:46
  75.9 6.0 %collective-permute-start.19 = (bf16[112,640]{1,0:T(8,128)(2,1)S(1)}, bf16[112,640]{1,0:T(8,128)(2,1)S(1)}, u32[]{:S(2)}, u32[]{:S(2)}) collective-permute-start(bf16[112,640]{1,0:T(8,128)(2,1)S(1)} %slice.7), channel_id=1, source_target_pairs={{2,0},{3,1},{0,2},{1,3},{6,4},{7,5},{4,6},{5,7},{10,8},{11,9},{8,1... | collective-permute-start | bytes 430088 | tf_op jit(solution)/shard_map/ppermute | solution.py:50
  76.1 5.7 %collective-permute-start.18 = (bf16[96,640]{1,0:T(8,128)(2,1)S(1)}, bf16[96,640]{1,0:T(8,128)(2,1)S(1)}, u32[]{:S(2)}, u32[]{:S(2)}) collective-permute-start(bf16[96,640]{1,0:T(8,128)(2,1)S(1)} %slice.6), channel_id=1, source_target_pairs={{2,0},{3,1},{0,2},{1,3},{6,4},{7,5},{4,6},{5,7},{10,8},{11,9},{8,1... | collective-permute-start | bytes 368648 | tf_op jit(solution)/shard_map/ppermute | solution.py:50
  85.1 21.1 %collective-permute-start.22 = (bf16[704,640]{1,0:T(8,128)(2,1)S(1)}, bf16[704,640]{1,0:T(8,128)(2,1)S(1)}, u32[]{:S(2)}, u32[]{:S(2)}) collective-permute-start(bf16[704,640]{1,0:T(8,128)(2,1)S(1)} %constant_dynamic-update-slice_fusion.4.refs_0_), channel_id=1, source_target_pairs={{2,0},{3,1},{0,2},{1,3},{6,4},{7,5},{4,6},{5,7},{10,8},{11,9},{8,1... | collective-permute-start | bytes 2703368 | tf_op jit(solution)/shard_map/ppermute | solution.py:50
  86.0 2.3 %collective-permute-start.23 = (bf16[208,640]{1,0:T(8,128)(2,1)S(1)}, bf16[208,640]{1,0:T(8,128)(2,1)S(1)}, u32[]{:S(2)}, u32[]{:S(2)}) collective-permute-start(bf16[208,640]{1,0:T(8,128)(2,1)S(1)} %get-tuple-element.58.refs_0_), channel_id=1, source_target_pairs={{1,0},{0,1},{3,2},{2,3},{5,4},{4,5},{7,6},{6,7},{9,8},{8,9},{11,10... | collective-permute-start | bytes 798728 | tf_op jit(solution)/shard_map/ppermute | solution.py:50
  86.8 1.6 %collective-permute-start.25 = (bf16[112,640]{1,0:T(8,128)(2,1)S(1)}, bf16[112,640]{1,0:T(8,128)(2,1)S(1)}, u32[]{:S(2)}, u32[]{:S(2)}) collective-permute-start(bf16[112,640]{1,0:T(8,128)(2,1)S(1)} %collective-permute-done.19.refs_2_), channel_id=1, source_target_pairs={{1,0},{0,1},{3,2},{2,3},{5,4},{4,5},{7,6},{6,7},{9,8},{8,9},{11,10... | collective-permute-start | bytes 430088 | tf_op jit(solution)/shard_map/ppermute | solution.py:50
  86.8 1.5 %collective-permute-start.24 = (bf16[96,640]{1,0:T(8,128)(2,1)S(1)}, bf16[96,640]{1,0:T(8,128)(2,1)S(1)}, u32[]{:S(2)}, u32[]{:S(2)}) collective-permute-start(bf16[96,640]{1,0:T(8,128)(2,1)S(1)} %collective-permute-done.18.refs_1_), channel_id=1, source_target_pairs={{1,0},{0,1},{3,2},{2,3},{5,4},{4,5},{7,6},{6,7},{9,8},{8,9},{11,10... | collective-permute-start | bytes 368648 | tf_op jit(solution)/shard_map/ppermute | solution.py:50
  89.1 17.9 %collective-permute-start.26 = (bf16[208,640]{1,0:T(8,128)(2,1)S(1)}, bf16[208,640]{1,0:T(8,128)(2,1)S(1)}, u32[]{:S(2)}, u32[]{:S(2)}) collective-permute-start(bf16[208,640]{1,0:T(8,128)(2,1)S(1)} %get-tuple-element.63), channel_id=1, source_target_pairs={{12,0},{13,1},{14,2},{15,3},{0,4},{1,5},{2,6},{3,7},{4,8},{5,9},{6... | collective-permute-start | bytes 798728 | tf_op jit(solution)/shard_map/ppermute | solution.py:46
  91.3 22.5 %collective-permute-start.27 = (bf16[208,640]{1,0:T(8,128)(2,1)S(1)}, bf16[208,640]{1,0:T(8,128)(2,1)S(1)}, u32[]{:S(2)}, u32[]{:S(2)}) collective-permute-start(bf16[208,640]{1,0:T(8,128)(2,1)S(1)} %get-tuple-element.64), channel_id=1, source_target_pairs={{8,0},{9,1},{10,2},{11,3},{12,4},{13,5},{14,6},{15,7},{0,8},{1,9},... | collective-permute-start | bytes 798728 | tf_op jit(solution)/shard_map/ppermute | solution.py:46
  92.8 22.4 %collective-permute-start.28 = (bf16[208,640]{1,0:T(8,128)(2,1)S(1)}, bf16[208,640]{1,0:T(8,128)(2,1)S(1)}, u32[]{:S(2)}, u32[]{:S(2)}) collective-permute-start(bf16[208,640]{1,0:T(8,128)(2,1)S(1)} %get-tuple-element.65), channel_id=1, source_target_pairs={{4,0},{5,1},{6,2},{7,3},{8,4},{9,5},{10,6},{11,7},{12,8},{13,9},{1... | collective-permute-start | bytes 798728 | tf_op jit(solution)/shard_map/ppermute | solution.py:46
  115.1 3.4 %collective-permute-start.29 = (bf16[176,2560]{1,0:T(8,128)(2,1)S(1)}, bf16[176,2560]{1,0:T(8,128)(2,1)S(1)}, u32[]{:S(2)}, u32[]{:S(2)}) collective-permute-start(bf16[176,2560]{1,0:T(8,128)(2,1)S(1)} %shard_map.118), channel_id=1, source_target_pairs={{1,0},{0,1},{3,2},{2,3},{5,4},{4,5},{7,6},{6,7},{9,8},{8,9},{11,10... | collective-permute-start | bytes 2703368 | tf_op jit(solution)/shard_map/ppermute | solution.py:50
